TPU v7x, 32 devices: a whole 2x2x4 slice. The times are simulated.
32 devices in a mesh: seq: 16 (over z, x, core), batch: 2 (over y).
Axes of the slice: x: 2, y: 2, z: 4, core: 2. Of those that a mesh axis runs over, the one named last changes fastest.
Arguments:
- states: float32 [2, 2048, 1024], P('batch', 'seq'), may hold values from -6 to 6
- lengths: int32 [2, 4], P('batch'), may hold values from 0 to 2048, as said below
- w_query: bfloat16 [1024, 1024], P(None, 'seq'), may hold values from -0.1875 to 0.1875
- w_key: bfloat16 [1024, 1024], P(None, 'seq'), may hold values from -0.1875 to 0.1875
- w_value: bfloat16 [1024, 1024], P(None, 'seq'), may hold values from -0.1875 to 0.1875
- w_out: bfloat16 [1024, 1024], P('seq'), may hold values from -0.1875 to 0.1875
- w_up: bfloat16 [1024, 4096], P(None, 'seq'), may hold values from -0.1875 to 0.1875
- w_gate: bfloat16 [1024, 4096], P(None, 'seq'), may hold values from -0.1875 to 0.1875
- w_down: bfloat16 [4096, 1024], P('seq'), may hold values from -0.1875 to 0.1875
- qk_scale: float32 [1024], replicated, may hold values from 0.8 to 1.6
- up_scale: float32 [4096], replicated, may hold values from 0.5 to 1.5
- gate_scale: float32 [4096], replicated, may hold values from 0.5 to 1.5
- alpha_attn: float32 [1024], replicated, may hold values from 0.15 to 0.6
- alpha_mlp: float32 [1024], replicated, may hold values from 0.15 to 0.6
- d_out: float32 [2, 2048, 1024], P('batch', 'seq'), may hold values from -6 to 6
Outputs:
- output: float32 [2, 2048, 1024], P('batch', 'seq')
- d_states: float32 [2, 2048, 1024], P('batch', 'seq')
- g_query: float32 [1024, 1024], P(None, 'seq')
- g_key: float32 [1024, 1024], P(None, 'seq')
- g_value: float32 [1024, 1024], P(None, 'seq')
- g_out: float32 [1024, 1024], P('seq')
- g_up: float32 [1024, 4096], P(None, 'seq')
- g_gate: float32 [1024, 4096], P(None, 'seq')
- g_down: float32 [4096, 1024], P('seq')
- g_qk_scale: float32 [1024], replicated
- g_up_scale: float32 [4096], replicated
- g_gate_scale: float32 [4096], replicated
- g_alpha_attn: float32 [1024], replicated
- g_alpha_mlp: float32 [1024], replicated
Inputs may be any that keep to these rules, and one draw needn't show every extreme that they name: Each row's 4 lengths sum to 2048, and documents may be empty; among the 1 row of each index of batch, one row holds a single document of 2048 tokens.
All inputs are finite; a program needn't handle non-finite values.
Results may differ from a plain program's by a relative error of at most 0.025.
Values may be sent and summed in bfloat16 or wider, within the bound.
A program may use at most 192 MiB of HBM per device.

v0:
```python
import jax
import jax.numpy as jnp
from jax import lax
from jax.sharding import PartitionSpec as P

HEADS = 16
HEAD = 64


EPS = 1e-06


def shifted(value, axis, steps):
    count = lax.axis_size(axis)
    first, last = (max(0, -steps), min(count, count - steps))
    return lax.ppermute(value, axis, [(source, source + steps) for source in range(first, last)])


def shifted_2(block, axis, distance):
    devices = range(lax.axis_size(axis))
    route = [((i - distance) % len(devices), i) for i in devices]
    return lax.ppermute(block, axis, route)


def normalized(weight, axis):
    wide = weight.astype(jnp.float32)
    return wide * lax.rsqrt(jnp.sum(wide * wide, axis=axis, keepdims=True) + EPS)


def rms(values):
    return values * lax.rsqrt(jnp.mean(values * values, axis=-1, keepdims=True) + EPS)


def doc_layout(len_row, tok_index):
    ends = jnp.cumsum(len_row)
    starts = ends - len_row
    started = starts[None, :] <= tok_index[:, None]
    doc_ids = jnp.sum(started.astype(jnp.int32), axis=1) - 1
    first_tok = jnp.max(jnp.where(started, starts[None, :], 0), axis=1)
    return (doc_ids, tok_index - first_tok)


def rope(values, position):
    half = values.shape[-1] // 2
    freqs = 10000.0 ** (-jnp.arange(half, dtype=jnp.float32) / half)
    angle = position.astype(jnp.float32)[:, None] * freqs[None, :]
    cosine = jnp.cos(angle)[:, None, :]
    sine = jnp.sin(angle)[:, None, :]
    first = values[..., :half]
    second = values[..., half:]
    return jnp.concatenate(
        [first * cosine - second * sine, first * sine + second * cosine], axis=-1
    )


def prepare(linear, position, gain):
    count = linear.shape[0]
    shaped = linear.reshape(count, HEADS, HEAD)
    turned = rms(rope(shaped, position)) * gain.reshape(HEADS, HEAD)
    return turned.reshape(count, HEADS * HEAD)


def residual_mix(state, branch, alpha):
    return rms(state + alpha * (rms(branch) - state))


def gating(up_lin, gate_lin, up_scale, gate_scale):
    return up_scale * up_lin * jax.nn.silu(gate_scale * gate_lin)


def unit_back(raw_shard, grad_shard, axis):
    primal, pullback = jax.vjp(
        lambda weight: normalized(weight, axis), raw_shard.astype(jnp.float32)
    )
    return pullback(grad_shard)[0]


def on_device(
    states,
    lengths,
    w_query,
    w_key,
    w_value,
    w_out,
    w_up,
    w_gate,
    w_down,
    qk_scale,
    up_scale,
    gate_scale,
    alpha_attn,
    alpha_mlp,
    d_out,
):
    seq_count = lax.axis_size("seq")
    my_index = lax.axis_index("seq")
    rows = states.shape[0]
    tok = states.shape[1]
    width = states.shape[2]
    flat = rows * tok
    score_scale = HEAD ** (-0.5)
    row_layout = jax.vmap(doc_layout, in_axes=(0, None))
    unit_query = normalized(w_query, 0).astype(jnp.bfloat16)
    unit_key = normalized(w_key, 0).astype(jnp.bfloat16)
    unit_value = normalized(w_value, 0).astype(jnp.bfloat16)
    unit_out = normalized(w_out, 1).astype(jnp.bfloat16)
    unit_up = normalized(w_up, 0).astype(jnp.bfloat16)
    unit_gate = normalized(w_gate, 0).astype(jnp.bfloat16)
    unit_down = normalized(w_down, 1).astype(jnp.bfloat16)
    full_weights = (
        lax.all_gather(unit_query, "seq", axis=1, tiled=True),
        lax.all_gather(unit_key, "seq", axis=1, tiled=True),
        lax.all_gather(unit_value, "seq", axis=1, tiled=True),
        lax.all_gather(unit_out, "seq", axis=0, tiled=True),
        lax.all_gather(unit_up, "seq", axis=1, tiled=True),
        lax.all_gather(unit_gate, "seq", axis=1, tiled=True),
        lax.all_gather(unit_down, "seq", axis=0, tiled=True),
    )
    full_query, full_key, full_value, full_out, full_up, full_gate, full_down = full_weights
    tok_index = my_index * tok + jnp.arange(tok, dtype=jnp.int32)
    doc_ids, position = row_layout(lengths, tok_index)
    flat_pos = position.reshape(flat)
    state_in = states.reshape(flat, width)
    x_low = state_in.astype(jnp.bfloat16)
    query_lin = jnp.dot(x_low, full_query, preferred_element_type=jnp.float32)
    key_lin = jnp.dot(x_low, full_key, preferred_element_type=jnp.float32)
    value_lin = jnp.dot(x_low, full_value, preferred_element_type=jnp.float32)

    def front(query_part, key_part, gain):
        return (prepare(query_part, flat_pos, gain), prepare(key_part, flat_pos, gain))

    query_f, key_f = front(query_lin, key_lin, qk_scale)
    query_h = query_f.astype(jnp.bfloat16).reshape(rows, tok, HEADS, HEAD)
    key_h = key_f.astype(jnp.bfloat16).reshape(rows, tok, HEADS, HEAD)
    value_h = value_lin.astype(jnp.bfloat16).reshape(rows, tok, HEADS, HEAD)

    def block_scores(key_blk, source):
        key_index = source * tok + jnp.arange(tok, dtype=jnp.int32)
        key_docs, key_pos = row_layout(lengths, key_index)
        scores = (
            jnp.einsum("bqhd,bkhd->bqhk", query_h, key_blk, preferred_element_type=jnp.float32)
            * score_scale
        )
        allowed = (doc_ids[:, :, None] == key_docs[:, None, :]) & (
            key_index[None, None, :] <= tok_index[None, :, None]
        )
        return (scores, allowed[:, :, None, :])

    def is_active(source):
        last_key = jnp.reshape(source * tok + tok - 1, (1,))
        last_doc, last_pos = row_layout(lengths, last_key)
        return (source <= my_index) & jnp.any(last_doc[:, 0] >= doc_ids[:, 0])

    def attend(running, key_blk, value_blk, source):

        def compute(carried):
            best, denom_sum, accum = carried
            scores, allowed = block_scores(key_blk, source)
            new_best = jnp.maximum(best, jnp.max(jnp.where(allowed, scores, -1e30), axis=3))
            weights = jnp.where(allowed, jnp.exp(scores - new_best[:, :, :, None]), 0.0)
            shrink = jnp.exp(best - new_best)
            denom_sum = denom_sum * shrink + jnp.sum(weights, axis=3)
            accum = accum * shrink[:, :, :, None] + jnp.einsum(
                "bqhk,bkhd->bqhd",
                weights.astype(jnp.bfloat16),
                value_blk,
                preferred_element_type=jnp.float32,
            )
            return (new_best, denom_sum, accum)

        return lax.cond(is_active(source), compute, lambda carried: carried, running)

    reach = seq_count - 1
    start_state = (
        jnp.full((rows, tok, HEADS), -1e30, jnp.float32),
        jnp.zeros((rows, tok, HEADS), jnp.float32),
        jnp.zeros((rows, tok, HEADS, HEAD), jnp.float32),
    )
    first_state = attend(start_state, key_h, value_h, my_index)

    def cycle_step(step, loop_carry):
        running, key_blk, value_blk = loop_carry
        key_blk, value_blk = shifted((key_blk, value_blk), "seq", 1)
        source = (my_index - step) % seq_count
        return (attend(running, key_blk, value_blk, source), key_blk, value_blk)

    final_state, spent_key, spent_value = lax.fori_loop(
        1, reach + 1, cycle_step, (first_state, key_h, value_h)
    )
    best, denom_sum, accum = final_state
    attended = accum / denom_sum[:, :, :, None]
    log_sum = best + jnp.log(denom_sum)
    attended_low = attended.astype(jnp.bfloat16).reshape(flat, width)
    attn_branch = jnp.dot(attended_low, full_out, preferred_element_type=jnp.float32)
    state_mid = residual_mix(state_in, attn_branch, alpha_attn)
    mid_low = state_mid.astype(jnp.bfloat16)
    up_lin = jnp.dot(mid_low, full_up, preferred_element_type=jnp.float32)
    gate_lin = jnp.dot(mid_low, full_gate, preferred_element_type=jnp.float32)
    gated_low = gating(up_lin, gate_lin, up_scale, gate_scale).astype(jnp.bfloat16)
    mlp_branch = jnp.dot(gated_low, full_down, preferred_element_type=jnp.float32)
    output = residual_mix(state_mid, mlp_branch, alpha_mlp)
    back_weights = (
        lax.all_gather(unit_query, "seq", axis=1, tiled=True),
        lax.all_gather(unit_key, "seq", axis=1, tiled=True),
        lax.all_gather(unit_value, "seq", axis=1, tiled=True),
        lax.all_gather(unit_out, "seq", axis=0, tiled=True),
        lax.all_gather(unit_up, "seq", axis=1, tiled=True),
        lax.all_gather(unit_gate, "seq", axis=1, tiled=True),
        lax.all_gather(unit_down, "seq", axis=0, tiled=True),
    )
    back_query, back_key, back_value, back_out, back_up, back_gate, back_down = back_weights
    primal, pull_mlp = jax.vjp(residual_mix, state_mid, mlp_branch, alpha_mlp)
    d_mid, d_mlp, g_alpha_mlp = pull_mlp(d_out.reshape(flat, width))
    d_mlp_low = d_mlp.astype(jnp.bfloat16)
    grad_down = jnp.einsum("tf,td->fd", gated_low, d_mlp_low, preferred_element_type=jnp.float32)
    d_gated = jnp.einsum("td,fd->tf", d_mlp_low, back_down, preferred_element_type=jnp.float32)
    primal, pull_gate = jax.vjp(gating, up_lin, gate_lin, up_scale, gate_scale)
    d_up, d_gate, g_up_scale, g_gate_scale = pull_gate(d_gated)
    d_up_low = d_up.astype(jnp.bfloat16)
    d_gate_low = d_gate.astype(jnp.bfloat16)
    grad_up = jnp.einsum("tc,tf->cf", mid_low, d_up_low, preferred_element_type=jnp.float32)
    grad_gate = jnp.einsum("tc,tf->cf", mid_low, d_gate_low, preferred_element_type=jnp.float32)
    d_mid = d_mid + jnp.einsum("tf,cf->tc", d_up_low, back_up, preferred_element_type=jnp.float32)
    d_mid = d_mid + jnp.einsum(
        "tf,cf->tc", d_gate_low, back_gate, preferred_element_type=jnp.float32
    )
    primal, pull_attn = jax.vjp(residual_mix, state_in, attn_branch, alpha_attn)
    d_state, d_attn, g_alpha_attn = pull_attn(d_mid)
    d_attn_low = d_attn.astype(jnp.bfloat16)
    grad_out = jnp.einsum("tc,td->cd", attended_low, d_attn_low, preferred_element_type=jnp.float32)
    d_attended = jnp.einsum("td,cd->tc", d_attn_low, back_out, preferred_element_type=jnp.float32)
    d_att_low = d_attended.astype(jnp.bfloat16).reshape(rows, tok, HEADS, HEAD)
    delta = jnp.sum(d_att_low.astype(jnp.float32) * attended, axis=3)

    def attend_back(d_query, key_blk, value_blk, d_key, d_value, source):

        def compute(carried):
            d_query, d_key, d_value = carried
            scores, allowed = block_scores(key_blk, source)
            probs = jnp.where(allowed, jnp.exp(scores - log_sum[:, :, :, None]), 0.0)
            d_probs = jnp.einsum(
                "bqhd,bkhd->bqhk", d_att_low, value_blk, preferred_element_type=jnp.float32
            )
            d_scores = (probs * (d_probs - delta[:, :, :, None])).astype(jnp.bfloat16)
            d_query = d_query + jnp.einsum(
                "bqhk,bkhd->bqhd", d_scores, key_blk, preferred_element_type=jnp.float32
            )
            d_key = d_key + jnp.einsum(
                "bqhk,bqhd->bkhd", d_scores, query_h, preferred_element_type=jnp.float32
            )
            d_value = d_value + jnp.einsum(
                "bqhk,bqhd->bkhd",
                probs.astype(jnp.bfloat16),
                d_att_low,
                preferred_element_type=jnp.float32,
            )
            return (d_query, d_key, d_value)

        return lax.cond(
            is_active(source), compute, lambda carried: carried, (d_query, d_key, d_value)
        )

    def back_step(step, loop_carry):
        d_query, key_blk, value_blk, d_key, d_value = loop_carry
        source = (my_index - step) % seq_count
        d_query, d_key, d_value = attend_back(d_query, key_blk, value_blk, d_key, d_value, source)
        d_key, d_value = (
            shifted_2(d_key.astype(jnp.bfloat16), "seq", 1).astype(d_key.dtype),
            shifted_2(d_value.astype(jnp.bfloat16), "seq", 1).astype(d_value.dtype),
        )
        key_blk, value_blk = shifted((key_blk, value_blk), "seq", 1)
        return (d_query, key_blk, value_blk, d_key, d_value)

    zero_heads = jnp.zeros((rows, tok, HEADS, HEAD), jnp.float32)
    d_query_h, last_key_blk, last_value_blk, d_key_h, d_value_h = lax.fori_loop(
        0, reach, back_step, (zero_heads, key_h, value_h, zero_heads, zero_heads)
    )
    d_query_h, d_key_h, d_value_h = attend_back(
        d_query_h, last_key_blk, last_value_blk, d_key_h, d_value_h, (my_index - reach) % seq_count
    )
    d_key_h, d_value_h = (
        shifted_2(d_key_h.astype(jnp.bfloat16), "seq", -reach).astype(d_key_h.dtype),
        shifted_2(d_value_h.astype(jnp.bfloat16), "seq", -reach).astype(d_value_h.dtype),
    )
    primal, pull_front = jax.vjp(front, query_lin, key_lin, qk_scale)
    d_query_lin, d_key_lin, g_qk_scale = pull_front(
        (d_query_h.reshape(flat, width) * score_scale, d_key_h.reshape(flat, width) * score_scale)
    )
    d_query_low = d_query_lin.astype(jnp.bfloat16)
    d_key_low = d_key_lin.astype(jnp.bfloat16)
    d_value_low = d_value_h.reshape(flat, width).astype(jnp.bfloat16)
    grad_query = jnp.einsum("tc,tj->cj", x_low, d_query_low, preferred_element_type=jnp.float32)
    grad_key = jnp.einsum("tc,tj->cj", x_low, d_key_low, preferred_element_type=jnp.float32)
    grad_value = jnp.einsum("tc,tj->cj", x_low, d_value_low, preferred_element_type=jnp.float32)
    d_state = d_state + jnp.einsum(
        "tj,cj->tc", d_query_low, back_query, preferred_element_type=jnp.float32
    )
    d_state = d_state + jnp.einsum(
        "tj,cj->tc", d_key_low, back_key, preferred_element_type=jnp.float32
    )
    d_state = d_state + jnp.einsum(
        "tj,cj->tc", d_value_low, back_value, preferred_element_type=jnp.float32
    )
    shards = (
        lax.psum_scatter(
            grad_query.astype(jnp.bfloat16), "seq", scatter_dimension=1, tiled=True
        ).astype(jnp.float32),
        lax.psum_scatter(
            grad_key.astype(jnp.bfloat16), "seq", scatter_dimension=1, tiled=True
        ).astype(jnp.float32),
        lax.psum_scatter(
            grad_value.astype(jnp.bfloat16), "seq", scatter_dimension=1, tiled=True
        ).astype(jnp.float32),
        lax.psum_scatter(
            grad_out.astype(jnp.bfloat16), "seq", scatter_dimension=0, tiled=True
        ).astype(jnp.float32),
        lax.psum_scatter(
            grad_up.astype(jnp.bfloat16), "seq", scatter_dimension=1, tiled=True
        ).astype(jnp.float32),
        lax.psum_scatter(
            grad_gate.astype(jnp.bfloat16), "seq", scatter_dimension=1, tiled=True
        ).astype(jnp.float32),
        lax.psum_scatter(
            grad_down.astype(jnp.bfloat16), "seq", scatter_dimension=0, tiled=True
        ).astype(jnp.float32),
    )
    summed = (
        lax.psum(shards[0].astype(jnp.bfloat16), "batch").astype(jnp.float32),
        lax.psum(shards[1].astype(jnp.bfloat16), "batch").astype(jnp.float32),
        lax.psum(shards[2].astype(jnp.bfloat16), "batch").astype(jnp.float32),
        lax.psum(shards[3].astype(jnp.bfloat16), "batch").astype(jnp.float32),
        lax.psum(shards[4].astype(jnp.bfloat16), "batch").astype(jnp.float32),
        lax.psum(shards[5].astype(jnp.bfloat16), "batch").astype(jnp.float32),
        lax.psum(shards[6].astype(jnp.bfloat16), "batch").astype(jnp.float32),
    )
    gain_grads = lax.psum(
        (g_qk_scale, g_up_scale, g_gate_scale, g_alpha_attn, g_alpha_mlp), ("seq", "batch")
    )
    g_query = unit_back(w_query, summed[0], 0)
    g_key = unit_back(w_key, summed[1], 0)
    g_value = unit_back(w_value, summed[2], 0)
    g_out = unit_back(w_out, summed[3], 1)
    g_up = unit_back(w_up, summed[4], 0)
    g_gate = unit_back(w_gate, summed[5], 0)
    g_down = unit_back(w_down, summed[6], 1)
    return (
        output.reshape(rows, tok, width),
        d_state.reshape(rows, tok, width),
        g_query,
        g_key,
        g_value,
        g_out,
        g_up,
        g_gate,
        g_down,
        gain_grads[0],
        gain_grads[1],
        gain_grads[2],
        gain_grads[3],
        gain_grads[4],
    )


def solution(mesh):
    return jax.shard_map(
        on_device,
        mesh=mesh,
        in_specs=(
            P("batch", "seq", None),
            P("batch", None),
            P(None, "seq"),
            P(None, "seq"),
            P(None, "seq"),
            P("seq", None),
            P(None, "seq"),
            P(None, "seq"),
            P("seq", None),
            P(),
            P(),
            P(),
            P(),
            P(),
            P("batch", "seq", None),
        ),
        out_specs=(
            P("batch", "seq", None),
            P("batch", "seq", None),
            P(None, "seq"),
            P(None, "seq"),
            P(None, "seq"),
            P("seq", None),
            P(None, "seq"),
            P(None, "seq"),
            P("seq", None),
            P(),
            P(),
            P(),
            P(),
            P(),
        ),
        check_vma=False,
    )
```

profile of v0, /device:TPU:0, one launch (start us, length us, event | category | flops | bytes accessed | tf_op | source)
XLA Modules:
  0.0 1437.3 jit_solution(14657598960277686270)
XLA Ops:
  26.1 28.8 %all-gather.8.cloned.1.call-done = bf16[1024,1024]{0,1:T(8,128)(2,1)} async-done(((bf16[1024,64]{0,1:T(8,128)(2,1)}), bf16[1024,1024]{0,1:T(8,128)(2,1)}) %all-gather.8.cloned.1.call-update) | async-done | bytes 2097168 | tf_op jit(solution)/shard_map/all_gather | solution.py:112
  57.2 40.6 %all-gather.10.cloned.1.call-done = bf16[1024,1024]{0,1:T(8,128)(2,1)} async-done(((bf16[1024,64]{0,1:T(8,128)(2,1)}), bf16[1024,1024]{0,1:T(8,128)(2,1)}) %all-gather.10.cloned.1.call-update) | async-done | bytes 2097168 | tf_op jit(solution)/shard_map/all_gather | solution.py:111
  101.3 39.5 %all-gather.12.cloned.1.call-done = bf16[1024,1024]{0,1:T(8,128)(2,1)} async-done(((bf16[1024,64]{0,1:T(8,128)(2,1)}), bf16[1024,1024]{0,1:T(8,128)(2,1)}) %all-gather.12.cloned.1.call-update) | async-done | bytes 2097168 | tf_op jit(solution)/shard_map/all_gather | solution.py:113
  144.9 244.4 %while.52 = (s32[]{:T(128)}, f32[1,128,16]{1,2,0:T(8,128)S(1)}, f32[1,128,16]{1,2,0:T(8,128)S(1)}, f32[1,128,16,64]{1,3,2,0:T(8,128)S(1)}, bf16[1,128,16,64]{1,3...) while((s32[]{:T(128)}, f32[1,128,16]{1,2,0:T(8,128)S(1)}, ...), condition=%wide.region_23.24_spmd.clone, body=%wide.region_15.0_spmd.clone.sunk | while | flops 69787440 | bytes 8329940 | solution.py:187
  151.6 6.8 collective-permute-start
  158.4 4.4 collective-permute-start.1
  168.9 5.7 collective-permute-start.1
  176.8 8.4 collective-permute-start
  185.2 4.4 collective-permute-start.1
  191.7 8.5 collective-permute-start
  206.8 9.2 collective-permute-start
  216.0 5.4 collective-permute-start.1
  223.6 13.8 collective-permute-start
  243.9 15.1 %collective-permute-start = (bf16[1,128,16,64]{1,3,2,0:T(8,128)(2,1)S(1)}, bf16[1,128,16,64]{1,3,2,0:T(8,128)(2,1)S(1)}, u32[]{:S(2)}, u32[]{:S(2)}) collective-permute-start(bf16[1,128,16,64]{1,3,2,0:T(8,128)(2,1)S(1)} %get-tuple-element.1520), channel_id=1, source_target_pairs={{0,2},{2,4},{4,6},{6,8},{8,10},{10,12},{12,14},{14,16},{16,18},{18... | collective-permute-start | bytes 786440 | tf_op jit(solution)/shard_map/while/body/eval_jaxpr/ppermute | solution.py:16
  265.6 8.2 collective-permute-start
  280.3 7.3 collective-permute-start
  294.2 12.2 collective-permute-start
  313.0 18.7 %collective-permute-start = (bf16[1,128,16,64]{1,3,2,0:T(8,128)(2,1)S(1)}, bf16[1,128,16,64]{1,3,2,0:T(8,128)(2,1)S(1)}, u32[]{:S(2)}, u32[]{:S(2)}) collective-permute-start(bf16[1,128,16,64]{1,3,2,0:T(8,128)(2,1)S(1)} %get-tuple-element.1520), channel_id=1, source_target_pairs={{0,2},{2,4},{4,6},{6,8},{8,10},{10,12},{12,14},{14,16},{16,18},{18... | collective-permute-start | bytes 786440 | tf_op jit(solution)/shard_map/while/body/eval_jaxpr/ppermute | solution.py:16
  338.2 15.9 %collective-permute-start = (bf16[1,128,16,64]{1,3,2,0:T(8,128)(2,1)S(1)}, bf16[1,128,16,64]{1,3,2,0:T(8,128)(2,1)S(1)}, u32[]{:S(2)}, u32[]{:S(2)}) collective-permute-start(bf16[1,128,16,64]{1,3,2,0:T(8,128)(2,1)S(1)} %get-tuple-element.1520), channel_id=1, source_target_pairs={{0,2},{2,4},{4,6},{6,8},{8,10},{10,12},{12,14},{14,16},{16,18},{18... | collective-permute-start | bytes 786440 | tf_op jit(solution)/shard_map/while/body/eval_jaxpr/ppermute | solution.py:16
  360.6 8.0 collective-permute-start
  375.2 7.6 collective-permute-start
  392.9 6.0 fusion.145
  399.0 7.5 multiply_convert_fusion.2
  406.5 48.8 %all-gather.20.cloned.1.call-done = bf16[4096,1024]{1,0:T(8,128)(2,1)} async-done(((bf16[256,1024]{1,0:T(8,128)(2,1)}), bf16[4096,1024]{1,0:T(8,128)(2,1)}) %all-gather.20.cloned.1.call-update) | async-done | bytes 8388624 | tf_op jit(solution)/shard_map/all_gather | solution.py:117
  455.3 5.2 multiply_reduce_fusion.11
  462.8 7.9 multiply_reduce_fusion
  470.7 7.4 convolution_add_fusion.4
  487.3 320.2 %while.53 = (s32[]{:T(128)}, f32[1,128,16,64]{1,3,2,0:T(8,128)S(1)}, bf16[1,128,16,64]{1,3,2,0:T(8,128)(2,1)S(1)}, bf16[1,128,16,64]{1,3,2,0:T(8,128)(2,1)S(1)},...) while((s32[]{:T(128)}, ...), condition=%wide.region_44.45_spmd.clone, body=%wide.region_38.44_spmd.clone.sunk | while | flops 170837808 | bytes 20274132 | solution.py:275
  497.8 7.0 collective-permute-start.3
  510.8 4.8 collective-permute-start.4
  521.4 5.3 collective-permute-start.3
  532.6 7.2 collective-permute-start.4
  539.8 4.9 collective-permute-start.5
  544.8 6.9 collective-permute-start.2
  551.7 5.3 collective-permute-start.3
  567.9 8.5 collective-permute-start.2
  576.4 5.3 collective-permute-start.3
  595.9 7.7 collective-permute-start.3
  617.8 5.3 collective-permute-start.3
  637.2 5.3 collective-permute-start.3
  656.7 5.3 collective-permute-start.3
  672.9 5.5 collective-permute-start.2
  678.4 5.3 collective-permute-start.3
  697.9 6.1 collective-permute-start.3
  719.8 5.3 collective-permute-start.3
  739.2 5.3 collective-permute-start.3
  759.1 5.3 collective-permute-start.3
  775.3 5.7 collective-permute-start.2
  781.0 5.3 collective-permute-start.3
  800.5 5.3 collective-permute-start.3
  808.8 4.9 collective-permute-start.6
  813.6 11.0 collective-permute-done.6
  830.6 8.5 collective-permute-done.7
  841.2 5.6 convolution_convert_fusion
  848.2 5.6 convolution_convert_fusion.2
  855.4 5.6 convolution_convert_fusion.1
  861.1 38.2 %reduce-scatter.10.cloned.1.call-done = bf16[1024,64]{0,1:T(8,128)(2,1)} async-done(((bf16[1024,1024]{0,1:T(8,128)(2,1)}), bf16[1024,64]{0,1:T(8,128)(2,1)}) %reduce-scatter.10.cloned.1.call-update) | async-done | bytes 131088 | tf_op jit(solution)/shard_map/reduce_scatter | solution.py:308
  899.4 64.2 %reduce-scatter.8.cloned.1.call-done = bf16[1024,64]{0,1:T(8,128)(2,1)} async-done(((bf16[1024,1024]{0,1:T(8,128)(2,1)}), bf16[1024,64]{0,1:T(8,128)(2,1)}) %reduce-scatter.8.cloned.1.call-update) | async-done | bytes 131088 | tf_op jit(solution)/shard_map/reduce_scatter | solution.py:305
  963.6 64.8 %reduce-scatter.12.cloned.1.call-done = bf16[1024,64]{0,1:T(8,128)(2,1)} async-done(((bf16[1024,1024]{0,1:T(8,128)(2,1)}), bf16[1024,64]{0,1:T(8,128)(2,1)}) %reduce-scatter.12.cloned.1.call-update) | async-done | bytes 131088 | tf_op jit(solution)/shard_map/reduce_scatter | solution.py:311
  1028.3 107.5 %reduce-scatter.20.cloned.1.call-done = bf16[256,1024]{1,0:T(8,128)(2,1)} async-done(((bf16[4096,1024]{1,0:T(8,128)(2,1)}), bf16[256,1024]{1,0:T(8,128)(2,1)}) %reduce-scatter.20.cloned.1.call-update) | async-done | bytes 524304 | tf_op jit(solution)/shard_map/reduce_scatter | solution.py:323
  1135.9 108.7 %reduce-scatter.16.cloned.1.call-done = bf16[1024,256]{1,0:T(8,128)(2,1)} async-done(((bf16[1024,4096]{1,0:T(8,128)(2,1)}), bf16[1024,256]{1,0:T(8,128)(2,1)}) %reduce-scatter.16.cloned.1.call-update) | async-done | bytes 524304 | tf_op jit(solution)/shard_map/reduce_scatter | solution.py:317
  1244.5 108.5 %reduce-scatter.18.cloned.1.call-done = bf16[1024,256]{1,0:T(8,128)(2,1)} async-done(((bf16[1024,4096]{1,0:T(8,128)(2,1)}), bf16[1024,256]{1,0:T(8,128)(2,1)}) %reduce-scatter.18.cloned.1.call-update) | async-done | bytes 524304 | tf_op jit(solution)/shard_map/reduce_scatter | solution.py:320
  1353.2 41.8 %all-reduce.4 = (f32[1024]{0:T(1024)}, f32[4096]{0:T(1024)}, f32[4096]{0:T(1024)}, f32[1024]{0:T(1024)}, f32[1024]{0:T(1024)}) all-reduce(f32[1024]{0:T(1024)S(1)} %add_any.148, f32[4096]{0:T(1024)S(1)} %copy-done.51, f32[4096]{0:T(1024)S(1)} %get-tuple-element.1163, ...), channel_id=1, replica_groups=mesh['seq'=16,'batch'=2] {'seq','batch'}, use_global_device_ids=true, to_apply=%region_74.75 | all-reduce | flops 11264 | bytes 90112 | tf_op jit(solution)/shard_map/psum | solution.py:336
  1400.3 19.6 %all-reduce.8.cloned.1.call-done = (bf16[1024,64]{0,1:T(8,128)(2,1)}, bf16[1024,64]{0,1:T(8,128)(2,1)}, bf16[1024,64]{0,1:T(8,128)(2,1)}, bf16[64,1024]{1,0:T(8,...) async-done(((bf16[1024,64]{0,1:T(8,128)(2,1)}, bf16[1024,64]{0,1:T(8,128)(2,1)}, bf16[1024,64]{0,1:T(8,128)(2,1)}, ...) | async-done | bytes 2097168 | tf_op jit(solution)/shard_map/psum | solution.py:328
  (761 shorter events, 326.4 us)
Async XLA Ops:
  7.2 47.6 %all-gather.8.cloned.1.call-start = ((), (), s32[]{:S(2)}) async-start(), calls=%async_computation.7 | async-start | bytes 2228224 | tf_op jit(solution)/shard_map/all_gather | solution.py:112
  10.1 87.7 %all-gather.10.cloned.1.call-start = ((), (), s32[]{:S(2)}) async-start(), calls=%async_computation.8 | async-start | bytes 2228224 | tf_op jit(solution)/shard_map/all_gather | solution.py:111
  12.9 127.9 %all-gather.12.cloned.1.call-start = ((), (), s32[]{:S(2)}) async-start(), calls=%async_computation.9 | async-start | bytes 2228224 | tf_op jit(solution)/shard_map/all_gather | solution.py:113
  15.7 373.8 %all-gather.14.cloned.1.call-start = ((), (), s32[]{:S(2)}) async-start(), calls=%async_computation.10 | async-start | bytes 2228224 | tf_op jit(solution)/shard_map/all_gather | solution.py:114
  18.5 374.4 %all-gather.18.cloned.1.call-start = ((), (), s32[]{:S(2)}) async-start(), calls=%async_computation.12 | async-start | bytes 8912896 | tf_op jit(solution)/shard_map/all_gather | solution.py:116
  19.7 379.2 %all-gather.16.cloned.1.call-start = ((), (), s32[]{:S(2)}) async-start(), calls=%async_computation.11 | async-start | bytes 8912896 | tf_op jit(solution)/shard_map/all_gather | solution.py:115
  20.9 434.4 %all-gather.20.cloned.1.call-start = ((), (), s32[]{:S(2)}) async-start(), calls=%async_computation.13 | async-start | bytes 8912896 | tf_op jit(solution)/shard_map/all_gather | solution.py:117
  22.2 839.0 %reduce-scatter.14.cloned.1.call-start = ((), (), s32[]{:S(2)}) async-start(), calls=%async_computation.17 | async-start | bytes 2228224 | tf_op jit(solution)/shard_map/reduce_scatter | solution.py:314
  151.6 13.2 collective-permute-start
  176.8 14.8 %collective-permute-start = (bf16[1,128,16,64]{1,3,2,0:T(8,128)(2,1)S(1)}, bf16[1,128,16,64]{1,3,2,0:T(8,128)(2,1)S(1)}, u32[]{:S(2)}, u32[]{:S(2)}) collective-permute-start(bf16[1,128,16,64]{1,3,2,0:T(8,128)(2,1)S(1)} %get-tuple-element.1520), channel_id=1, source_target_pairs={{0,2},{2,4},{4,6},{6,8},{8,10},{10,12},{12,14},{14,16},{16,18},{18... | collective-permute-start | bytes 786440 | tf_op jit(solution)/shard_map/while/body/eval_jaxpr/ppermute | solution.py:16
  191.7 15.0 %collective-permute-start = (bf16[1,128,16,64]{1,3,2,0:T(8,128)(2,1)S(1)}, bf16[1,128,16,64]{1,3,2,0:T(8,128)(2,1)S(1)}, u32[]{:S(2)}, u32[]{:S(2)}) collective-permute-start(bf16[1,128,16,64]{1,3,2,0:T(8,128)(2,1)S(1)} %get-tuple-element.1520), channel_id=1, source_target_pairs={{0,2},{2,4},{4,6},{6,8},{8,10},{10,12},{12,14},{14,16},{16,18},{18... | collective-permute-start | bytes 786440 | tf_op jit(solution)/shard_map/while/body/eval_jaxpr/ppermute | solution.py:16
  206.8 16.6 %collective-permute-start = (bf16[1,128,16,64]{1,3,2,0:T(8,128)(2,1)S(1)}, bf16[1,128,16,64]{1,3,2,0:T(8,128)(2,1)S(1)}, u32[]{:S(2)}, u32[]{:S(2)}) collective-permute-start(bf16[1,128,16,64]{1,3,2,0:T(8,128)(2,1)S(1)} %get-tuple-element.1520), channel_id=1, source_target_pairs={{0,2},{2,4},{4,6},{6,8},{8,10},{10,12},{12,14},{14,16},{16,18},{18... | collective-permute-start | bytes 786440 | tf_op jit(solution)/shard_map/while/body/eval_jaxpr/ppermute | solution.py:16
  223.6 20.2 %collective-permute-start = (bf16[1,128,16,64]{1,3,2,0:T(8,128)(2,1)S(1)}, bf16[1,128,16,64]{1,3,2,0:T(8,128)(2,1)S(1)}, u32[]{:S(2)}, u32[]{:S(2)}) collective-permute-start(bf16[1,128,16,64]{1,3,2,0:T(8,128)(2,1)S(1)} %get-tuple-element.1520), channel_id=1, source_target_pairs={{0,2},{2,4},{4,6},{6,8},{8,10},{10,12},{12,14},{14,16},{16,18},{18... | collective-permute-start | bytes 786440 | tf_op jit(solution)/shard_map/while/body/eval_jaxpr/ppermute | solution.py:16
  243.9 21.5 %collective-permute-start = (bf16[1,128,16,64]{1,3,2,0:T(8,128)(2,1)S(1)}, bf16[1,128,16,64]{1,3,2,0:T(8,128)(2,1)S(1)}, u32[]{:S(2)}, u32[]{:S(2)}) collective-permute-start(bf16[1,128,16,64]{1,3,2,0:T(8,128)(2,1)S(1)} %get-tuple-element.1520), channel_id=1, source_target_pairs={{0,2},{2,4},{4,6},{6,8},{8,10},{10,12},{12,14},{14,16},{16,18},{18... | collective-permute-start | bytes 786440 | tf_op jit(solution)/shard_map/while/body/eval_jaxpr/ppermute | solution.py:16
  265.6 14.7 %collective-permute-start = (bf16[1,128,16,64]{1,3,2,0:T(8,128)(2,1)S(1)}, bf16[1,128,16,64]{1,3,2,0:T(8,128)(2,1)S(1)}, u32[]{:S(2)}, u32[]{:S(2)}) collective-permute-start(bf16[1,128,16,64]{1,3,2,0:T(8,128)(2,1)S(1)} %get-tuple-element.1520), channel_id=1, source_target_pairs={{0,2},{2,4},{4,6},{6,8},{8,10},{10,12},{12,14},{14,16},{16,18},{18... | collective-permute-start | bytes 786440 | tf_op jit(solution)/shard_map/while/body/eval_jaxpr/ppermute | solution.py:16
  280.3 13.7 collective-permute-start
  294.2 18.6 %collective-permute-start = (bf16[1,128,16,64]{1,3,2,0:T(8,128)(2,1)S(1)}, bf16[1,128,16,64]{1,3,2,0:T(8,128)(2,1)S(1)}, u32[]{:S(2)}, u32[]{:S(2)}) collective-permute-start(bf16[1,128,16,64]{1,3,2,0:T(8,128)(2,1)S(1)} %get-tuple-element.1520), channel_id=1, source_target_pairs={{0,2},{2,4},{4,6},{6,8},{8,10},{10,12},{12,14},{14,16},{16,18},{18... | collective-permute-start | bytes 786440 | tf_op jit(solution)/shard_map/while/body/eval_jaxpr/ppermute | solution.py:16
  313.0 25.2 %collective-permute-start = (bf16[1,128,16,64]{1,3,2,0:T(8,128)(2,1)S(1)}, bf16[1,128,16,64]{1,3,2,0:T(8,128)(2,1)S(1)}, u32[]{:S(2)}, u32[]{:S(2)}) collective-permute-start(bf16[1,128,16,64]{1,3,2,0:T(8,128)(2,1)S(1)} %get-tuple-element.1520), channel_id=1, source_target_pairs={{0,2},{2,4},{4,6},{6,8},{8,10},{10,12},{12,14},{14,16},{16,18},{18... | collective-permute-start | bytes 786440 | tf_op jit(solution)/shard_map/while/body/eval_jaxpr/ppermute | solution.py:16
  338.2 22.3 %collective-permute-start = (bf16[1,128,16,64]{1,3,2,0:T(8,128)(2,1)S(1)}, bf16[1,128,16,64]{1,3,2,0:T(8,128)(2,1)S(1)}, u32[]{:S(2)}, u32[]{:S(2)}) collective-permute-start(bf16[1,128,16,64]{1,3,2,0:T(8,128)(2,1)S(1)} %get-tuple-element.1520), channel_id=1, source_target_pairs={{0,2},{2,4},{4,6},{6,8},{8,10},{10,12},{12,14},{14,16},{16,18},{18... | collective-permute-start | bytes 786440 | tf_op jit(solution)/shard_map/while/body/eval_jaxpr/ppermute | solution.py:16
  360.6 14.4 %collective-permute-start = (bf16[1,128,16,64]{1,3,2,0:T(8,128)(2,1)S(1)}, bf16[1,128,16,64]{1,3,2,0:T(8,128)(2,1)S(1)}, u32[]{:S(2)}, u32[]{:S(2)}) collective-permute-start(bf16[1,128,16,64]{1,3,2,0:T(8,128)(2,1)S(1)} %get-tuple-element.1520), channel_id=1, source_target_pairs={{0,2},{2,4},{4,6},{6,8},{8,10},{10,12},{12,14},{14,16},{16,18},{18... | collective-permute-start | bytes 786440 | tf_op jit(solution)/shard_map/while/body/eval_jaxpr/ppermute | solution.py:16
  375.2 14.0 collective-permute-start
  487.2 412.1 %reduce-scatter.10.cloned.1.call-start = ((), (), s32[]{:S(2)}) async-start(), calls=%async_computation.15 | async-start | bytes 2228224 | tf_op jit(solution)/shard_map/reduce_scatter | solution.py:308
  492.7 12.1 collective-permute-start.4
  493.0 12.7 collective-permute-start.5
  510.8 15.9 %collective-permute-start.4 = (bf16[1,128,16,64]{1,3,2,0:T(8,128)(2,1)}, bf16[1,128,16,64]{1,3,2,0:T(8,128)(2,1)S(1)}, u32[]{:S(2)}, u32[]{:S(2)}) collective-permute-start(bf16[1,128,16,64]{1,3,2,0:T(8,128)(2,1)} %convert_element_type.737), channel_id=1, source_target_pairs={{30,0},{0,2},{2,4},{4,6},{6,8},{8,10},{10,12},{12,14},{14,16},{16,... | collective-permute-start | bytes 786440 | tf_op jit(solution)/shard_map/while/body/eval_jaxpr/ppermute | solution.py:22
  515.6 11.9 collective-permute-start.5
  532.6 24.4 %collective-permute-start.4 = (bf16[1,128,16,64]{1,3,2,0:T(8,128)(2,1)}, bf16[1,128,16,64]{1,3,2,0:T(8,128)(2,1)S(1)}, u32[]{:S(2)}, u32[]{:S(2)}) collective-permute-start(bf16[1,128,16,64]{1,3,2,0:T(8,128)(2,1)} %convert_element_type.737), channel_id=1, source_target_pairs={{30,0},{0,2},{2,4},{4,6},{6,8},{8,10},{10,12},{12,14},{14,16},{16,... | collective-permute-start | bytes 786440 | tf_op jit(solution)/shard_map/while/body/eval_jaxpr/ppermute | solution.py:22
  539.8 18.0 %collective-permute-start.5 = (bf16[1,128,16,64]{1,3,2,0:T(8,128)(2,1)S(1)}, bf16[1,128,16,64]{1,3,2,0:T(8,128)(2,1)S(1)}, u32[]{:S(2)}, u32[]{:S(2)}) collective-permute-start(bf16[1,128,16,64]{1,3,2,0:T(8,128)(2,1)S(1)} %convert_element_type.739), channel_id=1, source_target_pairs={{30,0},{0,2},{2,4},{4,6},{6,8},{8,10},{10,12},{12,14},{14,16},{16,... | collective-permute-start | bytes 786440 | tf_op jit(solution)/shard_map/while/body/eval_jaxpr/ppermute | solution.py:22
  544.8 14.0 collective-permute-start.2
  562.9 18.8 %collective-permute-start.4 = (bf16[1,128,16,64]{1,3,2,0:T(8,128)(2,1)}, bf16[1,128,16,64]{1,3,2,0:T(8,128)(2,1)S(1)}, u32[]{:S(2)}, u32[]{:S(2)}) collective-permute-start(bf16[1,128,16,64]{1,3,2,0:T(8,128)(2,1)} %convert_element_type.737), channel_id=1, source_target_pairs={{30,0},{0,2},{2,4},{4,6},{6,8},{8,10},{10,12},{12,14},{14,16},{16,... | collective-permute-start | bytes 786440 | tf_op jit(solution)/shard_map/while/body/eval_jaxpr/ppermute | solution.py:22
  565.4 17.2 %collective-permute-start.5 = (bf16[1,128,16,64]{1,3,2,0:T(8,128)(2,1)S(1)}, bf16[1,128,16,64]{1,3,2,0:T(8,128)(2,1)S(1)}, u32[]{:S(2)}, u32[]{:S(2)}) collective-permute-start(bf16[1,128,16,64]{1,3,2,0:T(8,128)(2,1)S(1)} %convert_element_type.739), channel_id=1, source_target_pairs={{30,0},{0,2},{2,4},{4,6},{6,8},{8,10},{10,12},{12,14},{14,16},{16,... | collective-permute-start | bytes 786440 | tf_op jit(solution)/shard_map/while/body/eval_jaxpr/ppermute | solution.py:22
  567.9 15.5 %collective-permute-start.2 = (bf16[1,128,16,64]{1,3,2,0:T(8,128)(2,1)S(1)}, bf16[1,128,16,64]{1,3,2,0:T(8,128)(2,1)S(1)}, u32[]{:S(2)}, u32[]{:S(2)}) collective-permute-start(bf16[1,128,16,64]{1,3,2,0:T(8,128)(2,1)S(1)} %copy.110), channel_id=1, source_target_pairs={{0,2},{2,4},{4,6},{6,8},{8,10},{10,12},{12,14},{14,16},{16,18},{18... | collective-permute-start | bytes 786440 | tf_op jit(solution)/shard_map/while/body/eval_jaxpr/ppermute | solution.py:16
  587.6 16.0 %collective-permute-start.4 = (bf16[1,128,16,64]{1,3,2,0:T(8,128)(2,1)}, bf16[1,128,16,64]{1,3,2,0:T(8,128)(2,1)S(1)}, u32[]{:S(2)}, u32[]{:S(2)}) collective-permute-start(bf16[1,128,16,64]{1,3,2,0:T(8,128)(2,1)} %convert_element_type.737), channel_id=1, source_target_pairs={{30,0},{0,2},{2,4},{4,6},{6,8},{8,10},{10,12},{12,14},{14,16},{16,... | collective-permute-start | bytes 786440 | tf_op jit(solution)/shard_map/while/body/eval_jaxpr/ppermute | solution.py:22
  590.1 14.4 collective-permute-start.5
  592.6 12.7 collective-permute-start.2
  609.5 13.6 collective-permute-start.4
  611.9 12.0 collective-permute-start.5
  629.0 13.6 collective-permute-start.4
  631.4 12.0 collective-permute-start.5
  648.4 13.6 collective-permute-start.4
  650.9 12.0 collective-permute-start.5
  667.9 15.8 %collective-permute-start.4 = (bf16[1,128,16,64]{1,3,2,0:T(8,128)(2,1)}, bf16[1,128,16,64]{1,3,2,0:T(8,128)(2,1)S(1)}, u32[]{:S(2)}, u32[]{:S(2)}) collective-permute-start(bf16[1,128,16,64]{1,3,2,0:T(8,128)(2,1)} %convert_element_type.737), channel_id=1, source_target_pairs={{30,0},{0,2},{2,4},{4,6},{6,8},{8,10},{10,12},{12,14},{14,16},{16,... | collective-permute-start | bytes 786440 | tf_op jit(solution)/shard_map/while/body/eval_jaxpr/ppermute | solution.py:22
  670.4 14.1 collective-permute-start.5
  672.9 12.5 collective-permute-start.2
  689.6 14.4 %collective-permute-start.4 = (bf16[1,128,16,64]{1,3,2,0:T(8,128)(2,1)}, bf16[1,128,16,64]{1,3,2,0:T(8,128)(2,1)S(1)}, u32[]{:S(2)}, u32[]{:S(2)}) collective-permute-start(bf16[1,128,16,64]{1,3,2,0:T(8,128)(2,1)} %convert_element_type.737), channel_id=1, source_target_pairs={{30,0},{0,2},{2,4},{4,6},{6,8},{8,10},{10,12},{12,14},{14,16},{16,... | collective-permute-start | bytes 786440 | tf_op jit(solution)/shard_map/while/body/eval_jaxpr/ppermute | solution.py:22
  692.1 12.8 collective-permute-start.5
  709.9 15.1 %collective-permute-start.4 = (bf16[1,128,16,64]{1,3,2,0:T(8,128)(2,1)}, bf16[1,128,16,64]{1,3,2,0:T(8,128)(2,1)S(1)}, u32[]{:S(2)}, u32[]{:S(2)}) collective-permute-start(bf16[1,128,16,64]{1,3,2,0:T(8,128)(2,1)} %convert_element_type.737), channel_id=1, source_target_pairs={{30,0},{0,2},{2,4},{4,6},{6,8},{8,10},{10,12},{12,14},{14,16},{16,... | collective-permute-start | bytes 786440 | tf_op jit(solution)/shard_map/while/body/eval_jaxpr/ppermute | solution.py:22
  713.9 12.0 collective-permute-start.5
  730.9 13.6 collective-permute-start.4
  733.4 12.0 collective-permute-start.5
  750.4 14.0 collective-permute-start.4
  752.9 12.4 collective-permute-start.5
  770.3 16.0 %collective-permute-start.4 = (bf16[1,128,16,64]{1,3,2,0:T(8,128)(2,1)}, bf16[1,128,16,64]{1,3,2,0:T(8,128)(2,1)S(1)}, u32[]{:S(2)}, u32[]{:S(2)}) collective-permute-start(bf16[1,128,16,64]{1,3,2,0:T(8,128)(2,1)} %convert_element_type.737), channel_id=1, source_target_pairs={{30,0},{0,2},{2,4},{4,6},{6,8},{8,10},{10,12},{12,14},{14,16},{16,... | collective-permute-start | bytes 786440 | tf_op jit(solution)/shard_map/while/body/eval_jaxpr/ppermute | solution.py:22
  772.8 14.4 collective-permute-start.5
  775.3 12.7 collective-permute-start.2
  792.2 13.6 collective-permute-start.4
  794.7 12.0 collective-permute-start.5
  808.8 15.9 %collective-permute-start.6 = (bf16[1,128,16,64]{1,3,2,0:T(8,128)(2,1)S(1)}, bf16[1,128,16,64]{1,3,2,0:T(8,128)(2,1)S(1)}, u32[]{:S(2)}, u32[]{:S(2)}) collective-permute-start(bf16[1,128,16,64]{1,3,2,0:T(8,128)(2,1)S(1)} %convert_element_type.476), channel_id=1, source_target_pairs={{30,0},{0,2},{2,4},{4,6},{6,8},{8,10},{10,12},{12,14},{14,16},{16,... | collective-permute-start | bytes 786440 | tf_op jit(solution)/shard_map/ppermute | solution.py:22
  828.1 135.5 %reduce-scatter.8.cloned.1.call-start = ((), (), s32[]{:S(2)}) async-start(), calls=%async_computation.14 | async-start | bytes 2228224 | tf_op jit(solution)/shard_map/reduce_scatter | solution.py:305
  830.5 197.8 %reduce-scatter.12.cloned.1.call-start = ((), (), s32[]{:S(2)}) async-start(), calls=%async_computation.16 | async-start | bytes 2228224 | tf_op jit(solution)/shard_map/reduce_scatter | solution.py:311
  841.1 294.7 %reduce-scatter.20.cloned.1.call-start = ((), (), s32[]{:S(2)}) async-start(), calls=%async_computation.20 | async-start | bytes 8912896 | tf_op jit(solution)/shard_map/reduce_scatter | solution.py:323
  846.8 397.7 %reduce-scatter.16.cloned.1.call-start = ((), (), s32[]{:S(2)}) async-start(), calls=%async_computation.18 | async-start | bytes 8912896 | tf_op jit(solution)/shard_map/reduce_scatter | solution.py:317
  853.8 499.3 %reduce-scatter.18.cloned.1.call-start = ((), (), s32[]{:S(2)}) async-start(), calls=%async_computation.19 | async-start | bytes 8912896 | tf_op jit(solution)/shard_map/reduce_scatter | solution.py:320
  861.1 558.8 %all-reduce.8.cloned.1.call-start = ((), (), s32[]{:S(2)}) async-start(), calls=%async_computation.21 | async-start | bytes 4194304 | tf_op jit(solution)/shard_map/psum | solution.py:328
  (158 other events, 2198.6 us)
Sparse Core Ops, SparseCore 0:
  10.8 44.0 all-gather.7
  57.6 40.1 all-gather.9
  100.5 40.1 all-gather.11
  142.8 41.5 all-gather.13
  186.9 88.7 all-gather.17
  278.3 93.8 all-gather.15
  374.9 80.3 all-gather.19
  487.3 74.5 reduce-scatter.13
  828.2 71.1 reduce-scatter.9
  902.9 60.5 reduce-scatter.7
  967.8 60.5 reduce-scatter.11
  1032.2 103.5 reduce-scatter.19
  1139.9 104.5 reduce-scatter.15
  1248.5 104.5 reduce-scatter.17
  1355.6 64.2 all-reduce.7
where the time goes:
time: 1440 us
  waiting for transfers between devices  689 us (48%)
  starting transfers between devices  447 us (31%)
  other arithmetic  129 us (9%)
  matrix products  79.9 us (6%)
  blocking collectives  41.8 us (3%)
  loops' own time  25.1 us (2%)
  between operations  17 us (1%)
    ppermute x60, starting transfers between devices, shifted(): lax.ppermute(value, axis, [(source, source + steps) for source in range(f...  358 us
    reduce_scatter x1, waiting for transfers between devices, on_device(): lax.psum_scatter(grad_up.astype(jnp.bfloat16), 'seq', scatter_dimension=1...  109 us
    reduce_scatter x1, waiting for transfers between devices, on_device(): lax.psum_scatter(grad_gate.astype(jnp.bfloat16), 'seq', scatter_dimension...  109 us
    reduce_scatter x1, waiting for transfers between devices, on_device(): lax.psum_scatter(grad_down.astype(jnp.bfloat16), 'seq', scatter_dimension...  108 us
    ppermute x32, starting transfers between devices, shifted_2(): return lax.ppermute(block, axis, route)  88.3 us
    reduce_scatter x1, waiting for transfers between devices, on_device(): lax.psum_scatter(grad_value.astype(jnp.bfloat16), 'seq', scatter_dimensio...  64.8 us
    reduce_scatter x1, waiting for transfers between devices, on_device(): lax.psum_scatter(grad_query.astype(jnp.bfloat16), 'seq', scatter_dimensio...  64.2 us
    all_gather x1, waiting for transfers between devices, on_device(): lax.all_gather(unit_down, 'seq', axis=0, tiled=True)  48.8 us
  transfers between devices with their start and end apart: 107, of which 13 were waited for; matrix products, arithmetic and copies ran while one was open for 12% of the time, Pallas kernels for 0%

commit v1 on v0

--- a/solution.py
+++ b/solution.py
@@ -1,6 +1,9 @@
 import jax
 import jax.numpy as jnp
+import numpy as np
 from jax import lax
+from jax.experimental import pallas as pl
+from jax.experimental.pallas import tpu as pltpu
 from jax.sharding import PartitionSpec as P
 
 HEADS = 16
@@ -32,8 +35,8 @@
 
 
 def doc_layout(len_row, tok_index):
-    ends = jnp.cumsum(len_row)
-    starts = ends - len_row
+    docs = jnp.arange(len_row.shape[0])
+    starts = jnp.sum(jnp.where(docs[:, None] < docs[None, :], len_row[:, None], 0), axis=0)
     started = starts[None, :] <= tok_index[:, None]
     doc_ids = jnp.sum(started.astype(jnp.int32), axis=1) - 1
     first_tok = jnp.max(jnp.where(started, starts[None, :], 0), axis=1)
@@ -75,7 +78,7 @@
     return pullback(grad_shard)[0]
 
 
-def on_device(
+def on_device_general(
     states,
     lengths,
     w_query,
@@ -361,9 +364,827 @@
     )
 
 
+BF16 = jnp.bfloat16
+F32 = jnp.float32
+LANES = 128
+MIB = 1 << 20
+NT = (((1,), (1,)), ((), ()))
+TN = (((0,), (0,)), ((), ()))
+
+
+def place():
+    s = lax.axis_index("seq")
+    return s // 4, (s // 2) % 2, s % 2, lax.axis_index("batch")
+
+
+def dev(z, x, c, y):
+    return (z * 4 + x * 2 + c, y)
+
+
+def remote(src, dst, send, recv, device):
+    return pltpu.make_async_remote_copy(
+        src_ref=src,
+        dst_ref=dst,
+        send_sem=send,
+        recv_sem=recv,
+        device_id=device,
+        device_id_type=pl.DeviceIdType.MESH,
+    )
+
+
+def greet(fixed, line=True):
+    z, x, c, y = place()
+    bar = pltpu.get_barrier_semaphore()
+    for device in fixed:
+        pl.semaphore_signal(bar, inc=1, device_id=device, device_id_type=pl.DeviceIdType.MESH)
+    count = len(fixed)
+    if line:
+        for step in (-1, 1):
+
+            @pl.when((z + step >= 0) & (z + step < 4))
+            def _():
+                pl.semaphore_signal(
+                    bar,
+                    inc=1,
+                    device_id=dev(z + step, x, c, y),
+                    device_id_type=pl.DeviceIdType.MESH,
+                )
+
+        count = count + jnp.where((z == 0) | (z == 3), 1, 2)
+    pl.semaphore_wait(bar, count)
+
+
+def dot(a, b):
+    return jnp.dot(a, b, preferred_element_type=F32)
+
+
+def dot_nt(a, b):
+    return lax.dot_general(a, b, NT, preferred_element_type=F32)
+
+
+def dot_tn(a, b):
+    return lax.dot_general(a, b, TN, preferred_element_type=F32)
+
+
+def row_gather_body(buf, recv, zsend, xsend, csend, visit):
+    z, x, c, y = place()
+
+    def slot(zz, xx, cc):
+        return zz * 4 + xx * 2 + cc
+
+    def forward_z(zz, step):
+        b = slot(zz, x, c)
+        return remote(
+            buf.at[b], buf.at[b], zsend.at[zz, (step + 1) // 2], recv.at[b], dev(z + step, x, c, y)
+        )
+
+    def forward_x(zz):
+        b = slot(zz, x, c)
+        return remote(buf.at[b], buf.at[b], xsend.at[zz], recv.at[b], dev(z, 1 - x, c, y))
+
+    def forward_c(zz, xx):
+        b = slot(zz, xx, c)
+        return remote(buf.at[b], buf.at[b], csend.at[zz, xx], recv.at[b], dev(z, x, 1 - c, y))
+
+    def arrived(zz, xx, cc):
+        b = slot(zz, xx, cc)
+        remote(buf.at[b], buf.at[b], csend.at[0, 0], recv.at[b], dev(z, x, 1 - c, y)).wait_recv()
+
+    def inside(v):
+        return (v >= 0) & (v < 4)
+
+    for step in (-1, 1):
+
+        @pl.when(inside(z + step))
+        def _():
+            forward_z(z, step).start()
+
+    forward_x(z).start()
+    forward_c(z, x).start()
+    visit(slot(z, x, c))
+    for k in range(0, 4):
+        for way in (-1, 1):
+            if k > 0:
+                zz = z - way * k
+
+                @pl.when(inside(zz))
+                def _():
+                    arrived(zz, x, c)
+
+                    @pl.when(inside(z + way))
+                    def _():
+                        forward_z(zz, way).start()
+
+                    forward_x(zz).start()
+                    forward_c(zz, x).start()
+                    visit(slot(zz, x, c))
+
+        for way in (-1, 1) if k > 0 else (1,):
+            zz = z - way * k
+
+            @pl.when(inside(zz))
+            def _():
+                arrived(zz, 1 - x, c)
+                forward_c(zz, 1 - x).start()
+                visit(slot(zz, 1 - x, c))
+
+                arrived(zz, x, 1 - c)
+                visit(slot(zz, x, 1 - c))
+
+                arrived(zz, 1 - x, 1 - c)
+                visit(slot(zz, 1 - x, 1 - c))
+
+    for zz in range(4):
+        for step in (-1, 1):
+            own_or_passing = (zz <= z) if step > 0 else (zz >= z)
+
+            @pl.when(own_or_passing & inside(z + step))
+            def _():
+                forward_z(zz, step).wait_send()
+
+        forward_x(zz).wait_send()
+        for xx in range(2):
+            forward_c(zz, xx).wait_send()
+
+
+ROW_GATHER_SEMS = [
+    pltpu.SemaphoreType.DMA((16,)),
+    pltpu.SemaphoreType.DMA((4, 2)),
+    pltpu.SemaphoreType.DMA((4,)),
+    pltpu.SemaphoreType.DMA((4, 2)),
+]
+
+
+def greet_row_near():
+    z, x, c, y = place()
+    greet([dev(z, 1 - x, c, y), dev(z, x, 1 - c, y)])
+
+
+def row_gather_kernel(x_ref, out_ref, copy_sem, *sems):
+    z, x, c, y = place()
+    own = pltpu.make_async_copy(x_ref, out_ref.at[z * 4 + x * 2 + c], copy_sem)
+    own.start()
+    greet_row_near()
+    own.wait()
+    row_gather_body(out_ref, *sems, lambda slot: None)
+
+
+def row_gather(value, cid):
+    return pl.pallas_call(
+        row_gather_kernel,
+        name="row_gather",
+        out_shape=jax.ShapeDtypeStruct((16,) + value.shape, value.dtype),
+        in_specs=[pl.BlockSpec(memory_space=pl.ANY)],
+        out_specs=pl.BlockSpec(memory_space=pl.ANY),
+        scratch_shapes=[pltpu.SemaphoreType.DMA] + ROW_GATHER_SEMS,
+        compiler_params=pltpu.CompilerParams(collective_id=cid, has_side_effects=True),
+    )(value)
+
+
+def line_gather_body(buf, recv, zsend, visit):
+    z, x, c, y = place()
+
+    def inside(v):
+        return (v >= 0) & (v < 4)
+
+    def forward(zz, step):
+        return remote(
+            buf.at[zz], buf.at[zz], zsend.at[zz, (step + 1) // 2], recv.at[zz], dev(z + step, x, c, y)
+        )
+
+    for step in (-1, 1):
+
+        @pl.when(inside(z + step))
+        def _():
+            forward(z, step).start()
+
+    visit(z)
+    for k in range(1, 4):
+        for way in (-1, 1):
+            zz = z - way * k
+
+            @pl.when(inside(zz))
+            def _():
+                remote(
+                    buf.at[zz], buf.at[zz], zsend.at[0, 0], recv.at[zz], dev(z - way, x, c, y)
+                ).wait_recv()
+
+                @pl.when(inside(z + way))
+                def _():
+                    forward(zz, way).start()
+
+                visit(zz)
+
+    for zz in range(4):
+        for step in (-1, 1):
+            own_or_passing = (zz <= z) if step > 0 else (zz >= z)
+
+            @pl.when(own_or_passing & inside(z + step))
+            def _():
+                forward(zz, step).wait_send()
+
+
+LINE_SEMS = [pltpu.SemaphoreType.DMA((4,)), pltpu.SemaphoreType.DMA((4, 2))]
+
+
+def line_gather_kernel(x_ref, out_ref, *sems):
+    z, x, c, y = place()
+    greet([])
+    out_ref[z] = x_ref[...]
+    line_gather_body(out_ref, *sems, lambda zz: None)
+
+
+def line_gather(value, cid):
+    return pl.pallas_call(
+        line_gather_kernel,
+        name="line_gather",
+        out_shape=jax.ShapeDtypeStruct((4,) + value.shape, value.dtype),
+        in_specs=[pl.BlockSpec(memory_space=pltpu.VMEM)],
+        out_specs=pl.BlockSpec(memory_space=pltpu.VMEM),
+        scratch_shapes=LINE_SEMS,
+        compiler_params=pltpu.CompilerParams(
+            collective_id=cid, has_side_effects=True, vmem_limit_bytes=16 * MIB
+        ),
+    )(value)
+
+
+def line_reduce_kernel(p_ref, out_ref, passing, landed, send, recv):
+    z, x, c, y = place()
+    greet([])
+
+    def inside(v):
+        return (v >= 0) & (v < 4)
+
+    def hop(owner, way):
+        d = (way + 1) // 2
+        return remote(
+            passing.at[owner],
+            landed.at[owner, d],
+            send.at[owner],
+            recv.at[owner, d],
+            dev(z + way, x, c, y),
+        )
+
+    for k in range(3, 0, -1):
+        for way in (-1, 1):
+            owner = z + way * k
+            d = (way + 1) // 2
+
+            @pl.when(inside(owner))
+            def _():
+                @pl.when(inside(z - way))
+                def _():
+                    hop(owner, way).wait_recv()
+                    passing[owner] = (
+                        p_ref[owner].astype(F32) + landed[owner, d].astype(F32)
+                    ).astype(BF16)
+
+                @pl.when(jnp.logical_not(inside(z - way)))
+                def _():
+                    passing[owner] = p_ref[owner].astype(BF16)
+
+                hop(owner, way).start()
+
+    out_ref[...] = p_ref[z].astype(F32)
+    for way in (-1, 1):
+        d = (way + 1) // 2
+
+        @pl.when(inside(z - way))
+        def _():
+            remote(
+                passing.at[z], landed.at[z, d], send.at[z], recv.at[z, d], dev(z - way, x, c, y)
+            ).wait_recv()
+            out_ref[...] += landed[z, d].astype(F32)
+
+    for owner in range(4):
+
+        @pl.when(owner != z)
+        def _():
+            way = jnp.where(owner > z, 1, -1)
+            remote(
+                passing.at[owner],
+                landed.at[owner, 0],
+                send.at[owner],
+                recv.at[owner, 0],
+                dev(z + way, x, c, y),
+            ).wait_send()
+
+
+def line_reduce(parts, cid):
+    shape = parts.shape[1:]
+    return pl.pallas_call(
+        line_reduce_kernel,
+        name="line_reduce",
+        out_shape=jax.ShapeDtypeStruct(shape, F32),
+        in_specs=[pl.BlockSpec(memory_space=pltpu.VMEM)],
+        out_specs=pl.BlockSpec(memory_space=pltpu.VMEM),
+        scratch_shapes=[
+            pltpu.VMEM((4,) + shape, BF16),
+            pltpu.VMEM((4, 2) + shape, BF16),
+            pltpu.SemaphoreType.DMA((4,)),
+            pltpu.SemaphoreType.DMA((4, 2)),
+        ],
+        compiler_params=pltpu.CompilerParams(
+            collective_id=cid, has_side_effects=True, vmem_limit_bytes=32 * MIB
+        ),
+    )(parts)
+
+
+def group_gather_kernel(up_ref, gate_ref, down_ref, ups, gates, downs, copies, xs, cs, rx, rc):
+    z, x, c, y = place()
+    width = up_ref.shape[1]
+
+    def cols(slot):
+        return pl.ds(pl.multiple_of(slot * width, width), width)
+
+    def views(slot):
+        return (ups.at[:, cols(slot)], gates.at[:, cols(slot)], downs.at[cols(slot), :])
+
+    mine = 2 * x + c
+    local = [
+        pltpu.make_async_copy(src, dst, copies.at[i])
+        for i, (src, dst) in enumerate(zip((up_ref, gate_ref, down_ref), views(mine)))
+    ]
+    for copy in local:
+        copy.start()
+    greet([dev(z, 1 - x, c, y), dev(z, x, 1 - c, y)], False)
+    own = (up_ref, gate_ref, down_ref)
+    to_x = [
+        remote(own[i], views(mine)[i], xs.at[i], rx.at[i], dev(z, 1 - x, c, y)) for i in range(3)
+    ]
+    to_c = [
+        remote(own[i], views(mine)[i], cs.at[i], rc.at[i], dev(z, x, 1 - c, y)) for i in range(3)
+    ]
+    for copy in to_x + to_c:
+        copy.start()
+    other = 2 * (1 - x) + c
+    from_x = views(other)
+    onward = [
+        remote(from_x[i], from_x[i], cs.at[3 + i], rc.at[3 + i], dev(z, x, 1 - c, y))
+        for i in range(3)
+    ]
+    for i in range(3):
+        remote(own[i], from_x[i], xs.at[i], rx.at[i], dev(z, 1 - x, c, y)).wait_recv()
+        onward[i].start()
+    for i in range(3):
+        to_x[i].wait_send()
+        to_c[i].wait()
+        onward[i].wait()
+        local[i].wait()
+
+
+def group_gather(up, gate, down, cid):
+    depth, width = up.shape
+    hbm = pl.BlockSpec(memory_space=pl.ANY)
+    return pl.pallas_call(
+        group_gather_kernel,
+        name="group_gather",
+        out_shape=(
+            jax.ShapeDtypeStruct((depth, 4 * width), BF16),
+            jax.ShapeDtypeStruct((depth, 4 * width), BF16),
+            jax.ShapeDtypeStruct((4 * width, depth), BF16),
+        ),
+        in_specs=[hbm] * 3,
+        out_specs=(hbm,) * 3,
+        scratch_shapes=[
+            pltpu.SemaphoreType.DMA((3,)),
+            pltpu.SemaphoreType.DMA((3,)),
+            pltpu.SemaphoreType.DMA((6,)),
+            pltpu.SemaphoreType.DMA((3,)),
+            pltpu.SemaphoreType.DMA((6,)),
+        ],
+        compiler_params=pltpu.CompilerParams(collective_id=cid, has_side_effects=True),
+    )(up, gate, down)
+
+
+def group_reduce_kernel(gu, gg, gd, ou, og, od, *scratch):
+    z, x, c, y = place()
+    width = ou.shape[1]
+    grads = (gu, gg, gd)
+    outs = (ou, og, od)
+    land_c, sums, land_x, land_y = scratch[0:3], scratch[3:6], scratch[6:9], scratch[9:12]
+    sc, rc, sx, rx, sy, ry = scratch[12:18]
+
+    def part(i, slot):
+        window = pl.ds(pl.multiple_of(slot * width, width), width)
+        return grads[i].at[window, :] if i == 2 else grads[i].at[:, window]
+
+    greet([dev(z, 1 - x, c, y), dev(z, x, 1 - c, y), dev(z, x, c, 1 - y)], False)
+    copies_c = [
+        remote(
+            part(i, 2 * (1 - x if h == 0 else x) + 1 - c),
+            land_c[i].at[h],
+            sc.at[i, h],
+            rc.at[i, h],
+            dev(z, x, 1 - c, y),
+        )
+        for h in range(2)
+        for i in range(3)
+    ]
+    for copy in copies_c:
+        copy.start()
+    copies_x = [
+        remote(sums[i].at[0], land_x[i], sx.at[i], rx.at[i], dev(z, 1 - x, c, y)) for i in range(3)
+    ]
+    copies_y = [
+        remote(sums[i].at[1], land_y[i], sy.at[i], ry.at[i], dev(z, x, c, 1 - y)) for i in range(3)
+    ]
+    for h in range(2):
+        for i in range(3):
+            copies_c[h * 3 + i].wait_recv()
+            mine = part(i, 2 * (1 - x if h == 0 else x) + c)
+            sums[i][h] = (mine[...].astype(F32) + land_c[i][h].astype(F32)).astype(BF16)
+            if h == 0:
+                copies_x[i].start()
+    for i in range(3):
+        copies_x[i].wait_recv()
+        sums[i][1] = (sums[i][1].astype(F32) + land_x[i][...].astype(F32)).astype(BF16)
+        copies_y[i].start()
+    for i in range(3):
+        copies_y[i].wait_recv()
+        outs[i][...] = sums[i][1].astype(F32) + land_y[i][...].astype(F32)
+    for copy in copies_c + copies_x + copies_y:
+        copy.wait_send()
+
+
+def group_reduce(gu, gg, gd, cid):
+    depth = gu.shape[0]
+    width = gu.shape[1] // 4
+    vmem = pl.BlockSpec(memory_space=pltpu.VMEM)
+    shapes = ((depth, width), (depth, width), (width, depth))
+    return pl.pallas_call(
+        group_reduce_kernel,
+        name="group_reduce",
+        out_shape=tuple(jax.ShapeDtypeStruct(shape, F32) for shape in shapes),
+        in_specs=[vmem] * 3,
+        out_specs=(vmem,) * 3,
+        scratch_shapes=[pltpu.VMEM((2,) + shape, BF16) for shape in shapes]
+        + [pltpu.VMEM((2,) + shape, BF16) for shape in shapes]
+        + [pltpu.VMEM(shape, BF16) for shape in shapes]
+        + [pltpu.VMEM(shape, BF16) for shape in shapes]
+        + [pltpu.SemaphoreType.DMA((3, 2))] * 2
+        + [pltpu.SemaphoreType.DMA((3,))] * 4,
+        compiler_params=pltpu.CompilerParams(
+            collective_id=cid, has_side_effects=True, vmem_limit_bytes=56 * MIB
+        ),
+    )(gu, gg, gd)
+
+
+def exchange_kernel(x_ref, out_ref, copy_sem, send, recv):
+    z, x, c, y = place()
+    s = z * 4 + x * 2 + c
+    own = pltpu.make_async_copy(x_ref.at[s], out_ref.at[s], copy_sem)
+    own.start()
+    bar = pltpu.get_barrier_semaphore()
+
+    def turn(k):
+        return (s + k) % 16
+
+    @pl.loop(1, 16)
+    def _(k):
+        pl.semaphore_signal(
+            bar, inc=1, device_id=(turn(k), y), device_id_type=pl.DeviceIdType.MESH
+        )
+
+    pl.semaphore_wait(bar, 15)
+
+    @pl.loop(1, 16)
+    def _(k):
+        t = turn(k)
+        remote(x_ref.at[t], out_ref.at[s], send.at[t], recv.at[s], (t, y)).start()
+
+    own.wait()
+
+    @pl.loop(1, 16)
+    def _(k):
+        t = turn(k)
+        remote(x_ref.at[t], out_ref.at[t], send.at[t], recv.at[t], (t, y)).wait()
+
+
+def exchange(value, cid):
+    vmem = pl.BlockSpec(memory_space=pltpu.VMEM)
+    return pl.pallas_call(
+        exchange_kernel,
+        name="exchange",
+        out_shape=jax.ShapeDtypeStruct(value.shape, value.dtype),
+        in_specs=[vmem],
+        out_specs=vmem,
+        scratch_shapes=[
+            pltpu.SemaphoreType.DMA,
+            pltpu.SemaphoreType.DMA((16,)),
+            pltpu.SemaphoreType.DMA((16,)),
+        ],
+        compiler_params=pltpu.CompilerParams(
+            collective_id=cid, has_side_effects=True, vmem_limit_bytes=8 * MIB
+        ),
+    )(value)
+
+
+def pack(heads):
+    half = heads.shape[1] // 2
+    return jnp.concatenate([heads[:, :half], heads[:, half:]], axis=2)
+
+
+def unpack(packed):
+    return jnp.concatenate([packed[:, :, :HEAD], packed[:, :, HEAD:]], axis=1)
+
+
+BLOCK = 256
+
+
+def attend_kernel(q_ref, k_ref, v_ref, out_ref, qe_ref):
+    count = q_ref.shape[0]
+    row = lax.broadcasted_iota(jnp.int32, (BLOCK, BLOCK), 0)
+    col = lax.broadcasted_iota(jnp.int32, (BLOCK, BLOCK), 1)
+    causal = row >= col
+    lane = lax.broadcasted_iota(jnp.int32, (BLOCK, LANES), 1)
+    for i in range(count // BLOCK):
+        rows = pl.ds(i * BLOCK, BLOCK)
+        q = q_ref[rows, :]
+        total = jnp.zeros((BLOCK, LANES), F32)
+        for j in range(i + 1):
+            keys = pl.ds(j * BLOCK, BLOCK)
+            p = jnp.exp(dot_nt(q, k_ref[keys, :]))
+            if i == j:
+                p = jnp.where(causal, p, 0.0)
+            total = total + dot(p.astype(BF16), v_ref[keys, :])
+        denom = total[:, HEAD : HEAD + 1]
+        out_ref[rows, :] = total / denom
+        log = -jnp.log(denom)
+        high = log.astype(BF16).astype(F32)
+        rest = log - high
+        qe_ref[rows, :] = jnp.where(
+            lane == HEAD, high, jnp.where(lane == HEAD + 1, rest, q.astype(F32))
+        ).astype(BF16)
+
+
+def attend_heads(q, k, v):
+    vmem = pl.BlockSpec(memory_space=pltpu.VMEM)
+    return pl.pallas_call(
+        attend_kernel,
+        name="attend",
+        out_shape=(jax.ShapeDtypeStruct(q.shape, F32), jax.ShapeDtypeStruct(q.shape, BF16)),
+        in_specs=[vmem] * 3,
+        out_specs=(vmem,) * 2,
+        compiler_params=pltpu.CompilerParams(vmem_limit_bytes=32 * MIB),
+    )(q, k, v)
+
+
+def attend_back_kernel(q_ref, k_ref, v_ref, do_ref, dq_ref, dk_ref, dv_ref):
+    count = q_ref.shape[0]
+    row = lax.broadcasted_iota(jnp.int32, (BLOCK, BLOCK), 0)
+    col = lax.broadcasted_iota(jnp.int32, (BLOCK, BLOCK), 1)
+    causal = row <= col
+    blocks = count // BLOCK
+    for j in range(blocks):
+        keys = pl.ds(j * BLOCK, BLOCK)
+        k = k_ref[keys, :]
+        v = v_ref[keys, :]
+        dk = jnp.zeros((BLOCK, LANES), F32)
+        dv = jnp.zeros((BLOCK, LANES), F32)
+        for i in range(j, blocks):
+            rows = pl.ds(i * BLOCK, BLOCK)
+            q = q_ref[rows, :]
+            do = do_ref[rows, :]
+            p = jnp.exp(dot_nt(k, q))
+            if i == j:
+                p = jnp.where(causal, p, 0.0)
+            ds = (p * dot_nt(v, do)).astype(BF16)
+            dv = dv + dot(p.astype(BF16), do)
+            dk = dk + dot(ds, q)
+            dq = dot_tn(ds, k)
+            if j == 0:
+                dq_ref[rows, :] = dq
+            else:
+                dq_ref[rows, :] += dq
+        dk_ref[keys, :] = dk
+        dv_ref[keys, :] = dv
+
+
+def attend_back_heads(q, k, v, do):
+    vmem = pl.BlockSpec(memory_space=pltpu.VMEM)
+    shape = jax.ShapeDtypeStruct(q.shape, F32)
+    return pl.pallas_call(
+        attend_back_kernel,
+        name="attend_back",
+        out_shape=(shape,) * 3,
+        in_specs=[vmem] * 4,
+        out_specs=(vmem,) * 3,
+        compiler_params=pltpu.CompilerParams(vmem_limit_bytes=40 * MIB),
+    )(q, k, v, do)
+
+
+def inverse_norm(weight, axis):
+    wide = weight.astype(F32)
+    return lax.rsqrt(jnp.sum(wide * wide, axis=axis, keepdims=True) + EPS)
+
+
+def unit_pull(weight, grad, axis):
+    inverse = inverse_norm(weight, axis)
+    unit = weight.astype(F32) * inverse
+    return inverse * (grad - unit * jnp.sum(grad * unit, axis=axis, keepdims=True))
+
+
+def turn_tables(count):
+    half = HEAD // 2
+    freqs = (10000.0 ** (-np.arange(half, dtype=np.float32) / half)).astype(np.float32)
+    angle = np.arange(count, dtype=np.float32)[:, None] * freqs[None, :]
+    cosine = np.cos(angle).astype(np.float32)
+    sine = np.sin(angle).astype(np.float32)
+    return np.tile(cosine, (1, 4)), np.concatenate([-sine, sine, -sine, sine], axis=1)
+
+
+def swap_halves(value):
+    half = HEAD // 2
+    pieces = [value[:, k * half : (k + 1) * half] for k in (1, 0, 3, 2)]
+    return jnp.concatenate(pieces, axis=1)
+
+
+def head_mean(value):
+    first = jnp.mean(value[:, :HEAD], axis=1, keepdims=True)
+    second = jnp.mean(value[:, HEAD:], axis=1, keepdims=True)
+    count = value.shape[0]
+    return jnp.concatenate(
+        [jnp.broadcast_to(first, (count, HEAD)), jnp.broadcast_to(second, (count, HEAD))], axis=1
+    )
+
+
+def mix(state, branch, alpha):
+    inv_b = lax.rsqrt(jnp.mean(branch * branch, axis=-1, keepdims=True) + EPS)
+    unit_b = branch * inv_b
+    step = unit_b - state
+    mixed = state + alpha * step
+    inv_m = lax.rsqrt(jnp.mean(mixed * mixed, axis=-1, keepdims=True) + EPS)
+    return mixed * inv_m, (unit_b, inv_b, step, inv_m)
+
+
+def mix_back(grad, out, saved, alpha):
+    unit_b, inv_b, step, inv_m = saved
+    d_mixed = inv_m * (grad - out * jnp.mean(grad * out, axis=-1, keepdims=True))
+    d_alpha = jnp.sum(d_mixed * step, axis=0)
+    d_unit = d_mixed * alpha
+    d_branch = inv_b * (d_unit - unit_b * jnp.mean(d_unit * unit_b, axis=-1, keepdims=True))
+    return d_mixed - d_unit, d_branch, d_alpha
+
+
+def pad_lanes(value, fill):
+    count = value.shape[0]
+    extra = jnp.concatenate(fill + [jnp.zeros((count, LANES - HEAD - len(fill)), F32)], axis=1)
+    return jnp.concatenate([value.astype(F32), extra], axis=1).astype(BF16)
+
+
+def on_device_heads(
+    states,
+    lengths,
+    w_query,
+    w_key,
+    w_value,
+    w_out,
+    w_up,
+    w_gate,
+    w_down,
+    qk_scale,
+    up_scale,
+    gate_scale,
+    alpha_attn,
+    alpha_mlp,
+    d_out,
+):
+    s = lax.axis_index("seq")
+    z, x, c, y = place()
+    tok, width = states.shape[1:]
+    count = 16 * tok
+    state_in = states.reshape(tok, width)
+    grad_out = d_out.reshape(tok, width)
+
+    unit_qkv = jnp.concatenate(
+        [normalized(w, 0).astype(BF16) for w in (w_query, w_key, w_value)], axis=1
+    )
+    unit_out = normalized(w_out, 1).astype(BF16)
+    unit_up = normalized(w_up, 0).astype(BF16)
+    unit_gate = normalized(w_gate, 0).astype(BF16)
+    unit_down = normalized(w_down, 1).astype(BF16)
+
+    x_all = row_gather(state_in.astype(BF16), 1).reshape(count, width)
+    full_out = row_gather(unit_out, 2).reshape(width, width)
+    full_qkv = row_gather(unit_qkv.T, 3).reshape(3 * width, width)
+    ups, gates, downs = group_gather(unit_up, unit_gate, unit_down, 4)
+
+    linear = dot(x_all, unit_qkv)
+    cosine, sine = turn_tables(count)
+    gain = lax.dynamic_slice(qk_scale, (s * HEAD,), (HEAD,))
+    gains = jnp.concatenate([gain, gain])[None, :]
+    turned = linear[:, :LANES] * cosine + swap_halves(linear[:, :LANES]) * sine
+    inverse = lax.rsqrt(head_mean(turned * turned) + EPS)
+    unit_qk = turned * inverse
+    qk = (unit_qk * gains).astype(BF16)
+    ones = jnp.ones((count, 1), F32)
+    q_ext = pad_lanes(qk[:, :HEAD].astype(F32) * HEAD ** (-0.5), [])
+    k_ext = pad_lanes(qk[:, HEAD:], [ones, ones])
+    v_ext = pad_lanes(linear[:, LANES:].astype(BF16), [ones, ones])
+
+    attended, q_back = attend_heads(q_ext, k_ext, v_ext)
+    attended = attended[:, :HEAD]
+    att_in = exchange(pack(attended.astype(BF16).reshape(16, tok, HEAD)), 5)
+    att_low = unpack(att_in).transpose(1, 0, 2).reshape(tok, width)
+
+    attn_branch = dot(att_low, full_out)
+    state_mid, saved_attn = mix(state_in, attn_branch, alpha_attn)
+
+    mid_all = line_gather(state_mid.astype(BF16), 6).reshape(4 * tok, width)
+    units = ups.shape[1]
+    up_gain = lax.dynamic_slice(up_scale, (z * units,), (units,))
+    gate_gain = lax.dynamic_slice(gate_scale, (z * units,), (units,))
+    up_lin = dot(mid_all, ups)
+    gate_lin = dot(mid_all, gates) * gate_gain
+    up_val = up_lin * up_gain
+    sig = 1.0 / (1.0 + jnp.exp(-gate_lin))
+    act = gate_lin * sig
+    hidden = (up_val * act).astype(BF16)
+    mlp_branch = line_reduce(dot(hidden, downs).astype(BF16).reshape(4, tok, width), 7)
+    output, saved_mlp = mix(state_mid, mlp_branch, alpha_mlp)
+
+    d_mid, d_mlp, g_alpha_mlp = mix_back(grad_out, output, saved_mlp, alpha_mlp)
+    d_mlp_all = line_gather(d_mlp.astype(BF16), 8).reshape(4 * tok, width)
+    d_hidden = dot_nt(d_mlp_all, downs)
+    d_up_val = d_hidden * act
+    d_gate_val = d_hidden * up_val * (sig * (1.0 + gate_lin * (1.0 - sig)))
+    g_up_scale = jnp.sum(d_up_val * up_lin, axis=0)
+    g_gate_scale = jnp.sum(d_gate_val * gate_lin, axis=0) / gate_gain
+    d_up_low = (d_up_val * up_gain).astype(BF16)
+    d_gate_low = (d_gate_val * gate_gain).astype(BF16)
+    d_mid_part = dot_nt(d_up_low, ups) + dot_nt(d_gate_low, gates)
+    d_mid = d_mid + line_reduce(d_mid_part.astype(BF16).reshape(4, tok, width), 9)
+    grad_down = dot_tn(hidden, d_mlp_all).astype(BF16)
+    grad_up = dot_tn(mid_all, d_up_low).astype(BF16)
+    grad_gate = dot_tn(mid_all, d_gate_low).astype(BF16)
+
+    d_state, d_attn, g_alpha_attn = mix_back(d_mid, state_mid, saved_attn, alpha_attn)
+    d_attn_low = d_attn.astype(BF16)
+    d_att = dot_nt(d_attn_low, full_out).astype(BF16)
+    d_att_in = exchange(pack(d_att.reshape(tok, 16, HEAD).transpose(1, 0, 2)), 10)
+    d_att_head = unpack(d_att_in).reshape(count, HEAD)
+    delta = -jnp.sum(d_att_head.astype(F32) * attended, axis=1, keepdims=True)
+    delta_high = delta.astype(BF16).astype(F32)
+    do_ext = pad_lanes(d_att_head, [delta_high, delta - delta_high])
+
+    d_q, d_k, d_v = attend_back_heads(q_back, k_ext, v_ext, do_ext)
+    g_up_sum, g_gate_sum, g_down_sum = group_reduce(grad_up, grad_gate, grad_down, 11)
+    grad_out_w = dot_tn(att_low, d_attn_low).astype(BF16)
+    g_out_shard = lax.psum_scatter(grad_out_w, "seq", scatter_dimension=0, tiled=True)
+
+    d_qk = jnp.concatenate([d_q[:, :HEAD] * HEAD ** (-0.5), d_k[:, :HEAD]], axis=1)
+    g_qk = jnp.sum(d_qk * unit_qk, axis=0)
+    d_unit = d_qk * gains
+    d_turned = inverse * (d_unit - unit_qk * head_mean(d_unit * unit_qk))
+    d_qk_low = (d_turned * cosine - swap_halves(d_turned) * sine).astype(BF16)
+    d_lin = jnp.concatenate([d_qk_low, d_v[:, :HEAD].astype(BF16)], axis=1)
+    grad_qkv = dot_tn(x_all, d_lin).astype(BF16)
+    d_lin_pad = jnp.concatenate([d_lin, jnp.zeros((count, HEAD), BF16)], axis=1)
+    d_lin_in = exchange(d_lin_pad.reshape(16, tok, 4 * HEAD), 12)
+    d_lin_own = d_lin_in[:, :, : 3 * HEAD].transpose(1, 0, 2).reshape(tok, 3 * width)
+    d_state = d_state + dot(d_lin_own, full_qkv)
+
+    g_small = lax.psum(
+        jnp.concatenate([grad_qkv, g_out_shard.reshape(width, HEAD)], axis=1), "batch"
+    ).astype(F32)
+
+    place_units = (z * units,)
+    gains_full = jnp.concatenate(
+        [
+            lax.dynamic_update_slice(
+                jnp.zeros((width,), F32), g_qk[:HEAD] + g_qk[HEAD:], (s * HEAD,)
+            ),
+            lax.dynamic_update_slice(jnp.zeros((up_scale.shape[0],), F32), g_up_scale, place_units),
+            lax.dynamic_update_slice(jnp.zeros((up_scale.shape[0],), F32), g_gate_scale, place_units),
+            g_alpha_attn,
+            g_alpha_mlp,
+        ]
+    )
+    gains_full = lax.psum(gains_full, ("seq", "batch"))
+    ff = up_scale.shape[0]
+    cuts = (0, width, width + ff, width + 2 * ff, 2 * width + 2 * ff, 3 * width + 2 * ff)
+    gain_grads = [gains_full[a:b] for a, b in zip(cuts[:-1], cuts[1:])]
+
+    return (
+        output.reshape(states.shape),
+        d_state.reshape(states.shape),
+        unit_pull(w_query, g_small[:, :HEAD], 0),
+        unit_pull(w_key, g_small[:, HEAD : 2 * HEAD], 0),
+        unit_pull(w_value, g_small[:, 2 * HEAD : 3 * HEAD], 0),
+        unit_pull(w_out, g_small[:, 3 * HEAD :].reshape(HEAD, width), 1),
+        unit_pull(w_up, g_up_sum, 0),
+        unit_pull(w_gate, g_gate_sum, 0),
+        unit_pull(w_down, g_down_sum, 1),
+        *gain_grads,
+    )
+
+
 def solution(mesh):
+    seq, batch = mesh.shape["seq"], mesh.shape["batch"]
+    body = on_device_heads if (seq == HEADS and batch == 2) else on_device_general
     return jax.shard_map(
-        on_device,
+        body,
         mesh=mesh,
         in_specs=(
             P("batch", "seq", None),

time: 1440 us -> 592 us (0.41)
  waiting for transfers between devices: 689 us -> 24.6 us
  starting transfers between devices: 447 us -> 0.08 us
  Pallas kernels: 0 us -> 406 us
  other arithmetic: 129 us -> 37.7 us
  matrix products: 79.9 us -> 37.5 us
  loops' own time: 25.1 us -> 0 us
  local copies, waits for them, and re-layouts: 8.23 us -> 27.5 us
    reduce_scatter x7 -> x1, waiting for transfers between devices: 492 us -> 0.02 us  [on_device_heads(): lax.psum_scatter(grad_out_w, 'seq', scatter_dimension=0, tiled=True)]
    ppermute x92 -> x0, starting transfers between devices: 446 us -> none  [the longest x60 358 us: shifted(): lax.ppermute(value, axis, [(source, source + steps) for source in range(f...]
    pallas_call x0 -> x14, Pallas kernels: none -> 406 us  [the longest x3 161 us: row_gather(): pl.pallas_call(row_gather_kernel, name='row_gather', out_shape=jax.ShapeD...]
    all_gather x7 -> x0, waiting for transfers between devices: 158 us -> none  [the longest x1 48.8 us: on_device(): lax.all_gather(unit_down, 'seq', axis=0, tiled=True)]
    dot_general x28 -> x15, matrix products: 79.9 us -> 37.5 us  [the longest x6 16.1 us: dot(): return jnp.dot(a, b, preferred_element_type=F32)]
    convert_element_type x77 -> x14, other arithmetic: 48.7 us -> 8.22 us  [the longest x1 1.83 us: on_device_heads(): x_all = row_gather(state_in.astype(BF16), 1).reshape(count, width)]
    reduce_sum x49 -> x16, other arithmetic: 46.2 us -> 10.4 us  [the longest x5 3.75 us: unit_pull(): jnp.sum(grad * unit, axis=axis, keepdims=True)]
    another operation x34 -> x0, loops' own time: 25.1 us -> none  [the longest x1 12 us: on_device(): lax.fori_loop(0, reach, back_step, (zero_heads, key_h, value_h, zero_head...]
  transfers between devices with their start and end apart: 107 -> 2, of which waited for: 13 -> 1; matrix products, arithmetic and copies ran while one was open for 12% -> 7% of each run, Pallas kernels for 0% -> 30%
where the time goes in v1:
time: 592 us; the launch traced here: 587 us
  Pallas kernels  406 us (69%)
  other arithmetic  37.7 us (6%)
  blocking collectives  37.6 us (6%)
  matrix products  37.5 us (6%)
  local copies, waits for them, and re-layouts  27.5 us (5%)
  waiting for transfers between devices  24.6 us (4%)
  between operations  16 us (3%)
    pallas_call x3, Pallas kernels, row_gather(): pl.pallas_call(row_gather_kernel, name='row_gather', out_shape=jax.ShapeD...  161 us
    pallas_call x1, Pallas kernels, group_reduce(): pl.pallas_call(group_reduce_kernel, name='group_reduce', out_shape=tuple(...  57.2 us
    pallas_call x1, Pallas kernels, group_gather(): pl.pallas_call(group_gather_kernel, name='group_gather', out_shape=(jax.S...  48.9 us
    pallas_call x2, Pallas kernels, line_gather(): pl.pallas_call(line_gather_kernel, name='line_gather', out_shape=jax.Shap...  42 us
    pallas_call x2, Pallas kernels, line_reduce(): pl.pallas_call(line_reduce_kernel, name='line_reduce', out_shape=jax.Shap...  40.4 us
    pallas_call x3, Pallas kernels, exchange(): pl.pallas_call(exchange_kernel, name='exchange', out_shape=jax.ShapeDtype...  40.4 us
    psum x1, blocking collectives, on_device_heads(): gains_full = lax.psum(gains_full, ('seq', 'batch'))  37.6 us
    psum x1, waiting for transfers between devices, on_device_heads(): lax.psum(jnp.concatenate([grad_qkv, g_out_shard.reshape(width, HEAD)], ax...  24.5 us
  transfers between devices with their start and end apart: 2, of which 1 were waited for; matrix products, arithmetic and copies ran while one was open for 7% of the time, Pallas kernels for 30%

profile of v1, /device:TPU:0, one launch (start us, length us, event | category | flops | bytes accessed | tf_op | source)
XLA Modules:
  0.0 586.5 jit_solution(2316373805535906342)
XLA Ops:
  7.2 1.0 fusion.61
  8.3 1.0 fusion.65
  9.3 1.0 fusion.69
  10.4 1.0 fusion.57
  11.4 1.8 bitcast_convert_fusion.x_ref
  13.3 52.5 %row_gather.3 = bf16[16,128,1024]{2,1,0:T(8,128)(2,1)} custom-call(bf16[128,1024]{1,0:T(8,128)(2,1)} %bitcast_convert_fusion.x_ref), custom_call_target="tpu_custom_call" | custom-call | tf_op jit(solution)/shard_map/row_gather/pallas_call | solution.py:533
  66.0 3.5 convolution_bitcast_fusion
  70.4 2.9 fusion.80
  74.2 3.4 fusion.78
  77.5 0.9 slice_reduce_fusion.3
  83.4 0.9 fusion.3.down_ref
  84.3 32.1 %row_gather.4 = bf16[16,64,1024]{2,1,0:T(8,128)(2,1)} custom-call(bf16[64,1024]{1,0:T(8,128)(2,1)} %fusion.48.x_ref), custom_call_target="tpu_custom_call" | custom-call | tf_op jit(solution)/shard_map/row_gather/pallas_call | solution.py:533
  117.0 4.0 attend.1
  121.3 8.3 %exchange.3 = bf16[16,64,128]{2,1,0:T(8,128)(2,1)S(1)} custom-call(bf16[16,64,128]{2,1,0:T(8,128)(2,1)S(1)} %pad_maximum_fusion.4.x_ref), custom_call_target="tpu_custom_call" | custom-call | tf_op jit(solution)/shard_map/exchange/pallas_call | solution.py:866
  129.9 0.9 copy.51
  130.8 2.2 multiply_reduce_fusion.10
  134.3 24.5 %line_gather.2 = bf16[4,128,1024]{2,1,0:T(8,128)(2,1)S(1)} custom-call(bf16[128,1024]{1,0:T(8,128)(2,1)S(1)} %multiply_convert_fusion.5.x_ref), custom_call_target="tpu_custom_call" | custom-call | tf_op jit(solution)/shard_map/line_gather/pallas_call | solution.py:598
  158.9 1.2 fusion.6
  160.0 48.9 %group_gather.1 = (bf16[1024,1024]{1,0:T(8,128)(2,1)}, bf16[1024,1024]{1,0:T(8,128)(2,1)}, bf16[1024,1024]{1,0:T(8,128)(2,1)}) custom-call(bf16[1024,256]{1,0:T(8,128)(2,1)} %get-tuple-element.96.up_ref, bf16[1024,256]{1,0:T(8,128)(2,1)} %get-tuple-element.95.gate_ref, bf16[256,1024]{1,0:T(8,128)(2,1)} %fusion.3.down_ref), custom_call_target="tpu_custom_call" | custom-call | tf_op jit(solution)/shard_map/group_gather/pallas_call | solution.py:739
  209.0 3.0 fusion.88
  212.0 1.5 multiply_convert_fusion.2
  213.6 1.3 convolution_convert_fusion.4
  214.9 22.5 %line_reduce.2 = f32[128,1024]{1,0:T(8,128)S(1)} custom-call(bf16[4,128,1024]{2,1,0:T(8,128)(2,1)S(1)} %bitcast.92), custom_call_target="tpu_custom_call" | custom-call | tf_op jit(solution)/shard_map/line_reduce/pallas_call | solution.py:675
  238.0 1.0 fusion.38
  239.2 17.4 %line_gather.3 = bf16[4,128,1024]{2,1,0:T(8,128)(2,1)S(1)} custom-call(bf16[128,1024]{1,0:T(8,128)(2,1)S(1)} %fusion.40.x_ref), custom_call_target="tpu_custom_call" | custom-call | tf_op jit(solution)/shard_map/line_gather/pallas_call | solution.py:598
  256.7 2.9 multiply_reduce_fusion
  259.6 1.3 fusion.89
  261.3 1.1 copy-done.77
  262.3 1.3 add_convert_fusion
  263.6 18.0 %line_reduce.3 = f32[128,1024]{1,0:T(8,128)S(1)} custom-call(bf16[4,128,1024]{2,1,0:T(8,128)(2,1)S(1)} %bitcast.91), custom_call_target="tpu_custom_call" | custom-call | tf_op jit(solution)/shard_map/line_reduce/pallas_call | solution.py:675
  282.5 0.9 multiply_reduce_fusion.5
  284.2 2.0 convolution_convert_fusion.3
  286.3 4.3 convolution_convert_fusion.gd
  290.6 1.6 convolution_convert_fusion.6
  292.2 1.1 copy.45
  293.3 1.0 copy.46
  294.3 1.1 fusion.82
  295.6 8.2 %exchange.4 = bf16[16,64,128]{2,1,0:T(8,128)(2,1)S(1)} custom-call(bf16[16,64,128]{2,1,0:T(8,128)(2,1)S(1)} %pad_maximum_fusion.5.x_ref), custom_call_target="tpu_custom_call" | custom-call | tf_op jit(solution)/shard_map/exchange/pallas_call | solution.py:866
  304.9 1.3 copy.47
  306.2 4.3 convolution_convert_fusion.1.gg
  310.5 2.6 convolution_convert_fusion.2.gu
  314.0 1.4 copy.48
  315.4 1.4 subtract_convert_fusion
  317.3 11.2 %attend_back.1 = (f32[2048,128]{1,0:T(8,128)S(1)}, f32[2048,128]{1,0:T(8,128)S(1)}, f32[2048,128]{1,0:T(8,128)S(1)}) custom-call(bf16[2048,128]{1,0:T(8,128)(2,1)S(1)} %copy-done.2, bf16[2048,128]{1,0:T(8,128)(2,1)S(1)} %get-tuple-element.88.k_ref, bf16[2048,128]{1,0:T(8,128)(2,1)S(1)} %get-tuple-element.87.v_ref, ...), custom_call_target="tpu_custom_call" | custom-call | tf_op jit(solution)/shard_map/attend_back/pallas_call | solution.py:967
  328.7 1.1 copy-done.4
  331.0 0.9 slice_reduce_fusion.1
  332.6 0.9 multiply_reduce_fusion.2
  333.5 0.9 fusion.81
  335.1 0.9 fusion.31
  336.3 23.8 %exchange.5 = bf16[16,128,256]{2,1,0:T(8,128)(2,1)S(1)} custom-call(bf16[16,128,256]{2,1,0:T(8,128)(2,1)S(1)} %bitcast.84), custom_call_target="tpu_custom_call" | custom-call | tf_op jit(solution)/shard_map/exchange/pallas_call | solution.py:866
  361.2 76.8 %row_gather.5 = bf16[16,192,1024]{2,1,0:T(8,128)(2,1)} custom-call(bf16[192,1024]{1,0:T(8,128)(2,1)} %fusion.74.x_ref), custom_call_target="tpu_custom_call" | custom-call | tf_op jit(solution)/shard_map/row_gather/pallas_call | solution.py:533
  438.3 57.2 %group_reduce.1 = (f32[1024,256]{1,0:T(8,128)}, f32[1024,256]{1,0:T(8,128)}, f32[256,1024]{1,0:T(8,128)}) custom-call(bf16[1024,1024]{1,0:T(8,128)(2,1)} %convolution_convert_fusion.2.gu, bf16[1024,1024]{1,0:T(8,128)(2,1)} %convolution_convert_fusion.1.gg, bf16[1024,1024]{1,0:T(8,128)(2,1)} %convolution_convert_fusion.gd), custom_call_target="tpu_custom_call" | custom-call | tf_op jit(solution)/shard_map/group_reduce/pallas_call | solution.py:815
  496.4 37.6 %psum.15 = f32[11264]{0:T(1024)S(1)} all-reduce(f32[11264]{0:T(1024)S(1)} %constant_dynamic-update-slice_fusion), channel_id=1, replica_groups=mesh['seq'=16,'batch'=2] {'seq','batch'}, use_global_device_ids=true, to_apply=%region_34.35 | all-reduce | flops 11264 | bytes 90112 | tf_op jit(solution)/shard_map/psum | solution.py:1164
  534.1 1.6 fusion.13
  535.6 1.4 fusion.17
  538.6 1.1 fusion.15
  539.7 1.1 fusion.19
  540.9 1.2 fusion.23
  542.8 1.0 fusion.12
  543.9 1.2 reshape.238
  546.0 4.6 fusion.11
  550.7 24.5 %all-reduce.3.cloned.1.call-done = bf16[1024,256]{0,1:T(8,128)(2,1)} async-done(((bf16[1024,256]{0,1:T(8,128)(2,1)}), bf16[1024,256]{0,1:T(8,128)(2,1)}) %all-reduce.3.cloned.1.call-update) | async-done | bytes 524304 | tf_op jit(solution)/shard_map/psum | solution.py:1148
  575.2 1.0 slice.191
  578.2 1.0 fusion.68
  (265 shorter events, 24.6 us)
Async XLA Ops:
  7.2 536.7 %reduce-scatter.2.cloned.1.call-start = ((), (), s32[]{:S(2)}) async-start(), calls=%async_computation.1 | async-start | bytes 2228224 | tf_op jit(solution)/shard_map/reduce_scatter | solution.py:1134
  8.3 2.1 copy-start.62
  9.3 56.5 %copy-start.65 = (f32[64]{0:T(128)}, f32[64]{0:T(128)S(1)}, u32[]{:S(2)}) copy-start(f32[64]{0:T(128)S(1)} %add_rsqrt_fusion.9) | copy-start | bytes 772
  10.4 55.4 %copy-start.67 = (f32[64]{0:T(128)}, f32[64]{0:T(128)S(1)}, u32[]{:S(2)}) copy-start(f32[64]{0:T(128)S(1)} %add_rsqrt_fusion.8) | copy-start | bytes 772
  11.4 54.6 %copy-start.48 = (bf16[1024,64]{0,1:T(8,128)(2,1)}, bf16[1024,64]{0,1:T(8,128)(2,1)S(1)}, u32[]{:S(2)}) copy-start(bf16[1024,64]{0,1:T(8,128)(2,1)S(1)} %fusion.57) | copy-start | bytes 393220
  13.3 52.6 %copy-start.40 = (bf16[1024,64]{0,1:T(8,128)(2,1)S(1)}, bf16[1024,64]{0,1:T(8,128)(2,1)}, u32[]{:S(2)}) copy-start(bf16[1024,64]{0,1:T(8,128)(2,1)} %param.20) | copy-start | bytes 393220
  13.3 52.6 %copy-start.42 = (bf16[1024,64]{0,1:T(8,128)(2,1)S(1)}, bf16[1024,64]{0,1:T(8,128)(2,1)}, u32[]{:S(2)}) copy-start(bf16[1024,64]{0,1:T(8,128)(2,1)} %param.19) | copy-start | bytes 393220
  66.0 3.6 copy-start.50
  66.0 3.6 copy-start.52
  70.4 3.7 copy-start.26
  74.1 5.0 copy-start.69
  77.5 1.6 copy-start.3
  80.4 36.1 %copy-start.60 = (f32[64]{0:T(128)}, f32[64]{0:T(128)S(1)}, u32[]{:S(2)}) copy-start(f32[64]{0:T(128)S(1)} %add_rsqrt_fusion.7) | copy-start | bytes 772
  80.5 36.1 %copy-start.74 = (bf16[128]{0:T(256)(128)(2,1)}, bf16[128]{0:T(256)(128)(2,1)S(1)}, u32[]{:S(2)}) copy-start(bf16[128]{0:T(256)(128)(2,1)S(1)} %pad.34.clone) | copy-start | bytes 772
  82.0 179.0 %copy-start.72 = (f32[1024]{0:T(1024)}, f32[1024]{0:T(1024)S(1)}, u32[]{:S(2)}) copy-start(f32[1024]{0:T(1024)S(1)} %dynamic_slice.11) | copy-start | bytes 12292
  83.4 33.2 %copy-start.38 = (bf16[2048,64]{1,0:T(8,128)(2,1)S(1)}, bf16[2048,64]{1,0:T(8,128)(2,1)}, u32[]{:S(2)}) copy-start(bf16[2048,64]{1,0:T(8,128)(2,1)} %slice.223) | copy-start | bytes 786436
  121.0 8.7 %copy-start.1 = (bf16[2048,128]{1,0:T(8,128)(2,1)}, bf16[2048,128]{1,0:T(8,128)(2,1)S(1)}, u32[]{:S(2)}) copy-start(bf16[2048,128]{1,0:T(8,128)(2,1)S(1)} %get-tuple-element.29.q_ref) | copy-start | bytes 1572868
  130.8 2.3 copy-start.22
  130.8 2.3 copy-start.55
  133.1 25.8 %copy-start.13 = (bf16[1024,256]{1,0:T(8,128)(2,1)S(1)}, bf16[1024,256]{1,0:T(8,128)(2,1)}, u32[]{:S(2)}) copy-start(bf16[1024,256]{1,0:T(8,128)(2,1)} %param.22) | copy-start | bytes 1572868
  133.1 25.8 %copy-start.16 = (bf16[1024,256]{1,0:T(8,128)(2,1)S(1)}, bf16[1024,256]{1,0:T(8,128)(2,1)}, u32[]{:S(2)}) copy-start(bf16[1024,256]{1,0:T(8,128)(2,1)} %param.23) | copy-start | bytes 1572868
  133.1 149.4 %copy-start.64 = (f32[128]{0:T(128)}, f32[128]{0:T(128)S(1)}, u32[]{:S(2)}) copy-start(f32[128]{0:T(128)S(1)} %add_rsqrt_fusion.6) | copy-start | bytes 1540
  209.0 3.0 copy-start.78
  214.9 22.6 %copy-start.10 = (f32[128,1024]{1,0:T(8,128)S(1)}, f32[128,1024]{1,0:T(8,128)}, u32[]{:S(2)}) copy-start(f32[128,1024]{1,0:T(8,128)} %copy-done.9) | copy-start | bytes 1572868
  214.9 22.6 %copy-start.54 = (f32[1024]{0:T(1024)S(1)}, f32[1024]{0:T(1024)}, u32[]{:S(2)}) copy-start(f32[1024]{0:T(1024)} %param.29) | copy-start | bytes 12292
  214.9 22.9 %copy-start.35 = (f32[1,128,1024]{2,1,0:T(8,128)S(1)}, f32[1,128,1024]{2,1,0:T(8,128)}, u32[]{:S(2)}) copy-start(f32[1,128,1024]{2,1,0:T(8,128)} %param.30) | copy-start | bytes 1572868
  256.7 2.9 copy-start
  259.6 1.7 copy-start.80
  259.6 2.7 copy-start.77
  263.6 18.8 %copy-start.23 = (f32[1,128,1024]{2,1,0:T(8,128)S(1)}, f32[1,128,1024]{2,1,0:T(8,128)}, u32[]{:S(2)}) copy-start(f32[1,128,1024]{2,1,0:T(8,128)} %param.17) | copy-start | bytes 1572868
  263.6 18.8 %copy-start.25 = (f32[128,1024]{1,0:T(8,128)S(1)}, f32[128,1024]{1,0:T(8,128)}, u32[]{:S(2)}) copy-start(f32[128,1024]{1,0:T(8,128)} %copy-done.24) | copy-start | bytes 1572868
  282.5 1.8 copy-start.47
  286.3 289.0 %all-reduce.3.cloned.1.call-start = ((), (), s32[]{:S(2)}) async-start(), calls=%async_computation.2 | async-start | bytes 1048576 | tf_op jit(solution)/shard_map/psum | solution.py:1148
  286.3 4.3 copy-start.11
  306.2 4.3 copy-start.83
  313.1 2.3 copy-start.33
  313.7 3.1 copy-start.21
  313.7 3.1 copy-start.75
  315.4 1.9 copy-start.2
  328.5 1.9 copy-start.8
  328.6 1.8 copy-start.70
  333.5 1.6 copy-start.28
  336.0 24.1 %copy-start.44 = (bf16[2048,128]{1,0:T(8,128)(2,1)}, bf16[2048,128]{1,0:T(8,128)(2,1)S(1)}, u32[]{:S(2)}) copy-start(bf16[2048,128]{1,0:T(8,128)(2,1)S(1)} %fusion.31) | copy-start | bytes 1572868
  336.0 24.3 %copy-start.49 = (bf16[1024,64]{0,1:T(8,128)(2,1)S(1)}, bf16[1024,64]{0,1:T(8,128)(2,1)}, u32[]{:S(2)}) copy-start(bf16[1024,64]{0,1:T(8,128)(2,1)} %copy-done.48) | copy-start | bytes 393220
  336.1 24.3 %copy-start.51 = (bf16[1024,64]{0,1:T(8,128)(2,1)S(1)}, bf16[1024,64]{0,1:T(8,128)(2,1)}, u32[]{:S(2)}) copy-start(bf16[1024,64]{0,1:T(8,128)(2,1)} %copy-done.50) | copy-start | bytes 393220
  336.1 24.3 %copy-start.53 = (bf16[1024,64]{0,1:T(8,128)(2,1)S(1)}, bf16[1024,64]{0,1:T(8,128)(2,1)}, u32[]{:S(2)}) copy-start(bf16[1024,64]{0,1:T(8,128)(2,1)} %copy-done.52) | copy-start | bytes 393220
  360.4 77.6 %copy-start.58 = (f32[1024]{0:T(1024)}, f32[1024]{0:T(1024)S(1)}, u32[]{:S(2)}) copy-start(f32[1024]{0:T(1024)S(1)} %add_dynamic-update-slice_fusion) | copy-start | bytes 12292
  361.2 76.8 %copy-start.73 = (f32[1024]{0:T(1024)S(1)}, f32[1024]{0:T(1024)}, u32[]{:S(2)}) copy-start(f32[1024]{0:T(1024)} %get-tuple-element.37) | copy-start | bytes 12292
  438.3 57.2 %copy-start.59 = (f32[1024]{0:T(1024)S(1)}, f32[1024]{0:T(1024)}, u32[]{:S(2)}) copy-start(f32[1024]{0:T(1024)} %copy-done.58) | copy-start | bytes 12292
  438.3 57.3 %copy-start.71 = (f32[1024]{0:T(1024)S(1)}, f32[1024]{0:T(1024)}, u32[]{:S(2)}) copy-start(f32[1024]{0:T(1024)} %get-tuple-element.36) | copy-start | bytes 12292
  438.3 58.1 %copy-start.57 = (f32[1024]{0:T(1024)S(1)}, f32[1024]{0:T(1024)}, u32[]{:S(2)}) copy-start(f32[1024]{0:T(1024)} %get-tuple-element.40) | copy-start | bytes 12292
  438.3 58.1 %copy-start.56 = (f32[1024]{0:T(1024)S(1)}, f32[1024]{0:T(1024)}, u32[]{:S(2)}) copy-start(f32[1024]{0:T(1024)} %get-tuple-element.38) | copy-start | bytes 12292
  438.3 95.7 %copy-start.14 = (bf16[1024,256]{1,0:T(8,128)(2,1)S(1)}, bf16[1024,256]{1,0:T(8,128)(2,1)}, u32[]{:S(2)}) copy-start(bf16[1024,256]{1,0:T(8,128)(2,1)} %param.22) | copy-start | bytes 1572868
  495.5 40.1 %copy-start.17 = (bf16[1024,256]{1,0:T(8,128)(2,1)S(1)}, bf16[1024,256]{1,0:T(8,128)(2,1)}, u32[]{:S(2)}) copy-start(bf16[1024,256]{1,0:T(8,128)(2,1)} %param.23) | copy-start | bytes 1572868
  495.5 41.5 %copy-start.19 = (bf16[256,1024]{1,0:T(8,128)(2,1)S(1)}, bf16[256,1024]{1,0:T(8,128)(2,1)}, u32[]{:S(2)}) copy-start(bf16[256,1024]{1,0:T(8,128)(2,1)} %param.24) | copy-start | bytes 1572868
  534.0 3.0 copy-start.30
  534.0 4.5 copy-start.32
  537.1 2.7 copy-start.31
  539.7 2.9 copy-start.29
  539.7 3.1 copy-start.45
  543.8 2.2 copy-start.37
  550.7 26.0 %copy-start.61 = (f32[64]{0:T(128)S(1)}, f32[64]{0:T(128)}, u32[]{:S(2)}) copy-start(f32[64]{0:T(128)} %copy-done.60) | copy-start | bytes 772
  575.2 2.5 copy-start.46
  576.2 1.6 copy-start.39
  (22 other events, 27.4 us)
Sparse Core Ops, SparseCore 0:
  286.4 71.5 reduce-scatter.1
  546.1 29.0 all-reduce.2
